TPU v7x, 32 devices: a whole 2x2x4 slice. The times are simulated.
32 devices in a mesh: dp: 4 (over x, core), expert: 4 (over z), tensor: 2 (over y).
Axes of the slice: x: 2, y: 2, z: 4, core: 2. Of those that a mesh axis runs over, the one named last changes fastest.
Arguments:
- x_in: bfloat16 [4096, 1536], P(('dp', 'expert')), may hold values from -6 to 6
- segments: int32 [4096], P('dp'), may hold values from 0 to 1023, as said below
- chosen: int32 [4096, 8], P(('dp', 'expert')), may hold values from 0 to 39, all different within a row; in each aligned block of 256 rows (0 to 255, 256 to 511, ...) at most 80 rows name the same one
- out_grad: bfloat16 [4096, 1536], P(('dp', 'expert')), may hold values from -6 to 6
- norm1_gain: float32 [1536], replicated, may hold values from 0.5 to 1.5
- w_query: bfloat16 [1536, 1536], P(None, 'tensor'), may hold values from -0.3125 to 0.3125
- w_key: bfloat16 [1536, 512], P(None, 'tensor'), may hold values from -0.15625 to 0.15625
- w_value: bfloat16 [1536, 512], P(None, 'tensor'), may hold values from -0.15625 to 0.15625
- w_out: bfloat16 [1536, 1536], P('tensor'), may hold values from -0.625 to 0.625
- norm2_gain: float32 [1536], replicated, may hold values from 0.5 to 1.5
- w_router: bfloat16 [1536, 40], replicated, may hold values from -0.078125 to 0.078125
- w_gate: bfloat16 [40, 1536, 512], P('expert', None, 'tensor'), may hold values from -0.15625 to 0.15625
- w_up: bfloat16 [40, 1536, 512], P('expert', None, 'tensor'), may hold values from -0.15625 to 0.15625
- w_down: bfloat16 [40, 512, 1536], P('expert', 'tensor'), may hold values from -1 to 1
Outputs:
- block_out: bfloat16 [4096, 1536], P(('dp', 'expert'), 'tensor')
- input_grad: float32 [4096, 1536], P(('dp', 'expert'))
- grad_norm1: float32 [1536], P(('dp', 'expert'))
- grad_query: float32 [1536, 1536], P(('dp', 'expert'), 'tensor')
- grad_key: float32 [1536, 512], P(('dp', 'expert'), 'tensor')
- grad_value: float32 [1536, 512], P(('dp', 'expert'), 'tensor')
- grad_out: float32 [1536, 1536], P('tensor', ('dp', 'expert'))
- grad_norm2: float32 [1536], P(('dp', 'expert'))
- grad_router: float32 [1536, 40], P(('dp', 'expert'))
- grad_gate: float32 [40, 1536, 512], P('expert', 'dp', 'tensor')
- grad_up: float32 [40, 1536, 512], P('expert', 'dp', 'tensor')
- grad_down: float32 [40, 512, 1536], P('expert', 'tensor', 'dp')
Inputs may be any that keep to these rules, and one draw needn't show every extreme that they name: `segments`: document numbers never fall along a sequence, and the last token of every sequence carries 1024 - 1; documents do not attend to each other. `chosen`: each token names 8 different experts; among the tokens of one device no expert is named by more than 80 of them.
All inputs are finite; a program needn't handle non-finite values.
Results may differ from a plain program's by a relative error of at most 0.022.
Values may be sent and summed in bfloat16 or wider, within the bound.
No kernel may reach another device: no remote copies, remote signals or barrier semaphores. Data moves between devices by JAX's collectives and lax.ppermute only.
A program may use at most 320 MiB of HBM per device.

v0:
```python
import functools

import jax
import jax.numpy as jnp
import numpy as np
from jax import lax
from jax.experimental import pallas as pl
from jax.experimental.pallas import tpu as pltpu
from jax.sharding import PartitionSpec as P

HEAD_DIM = 64
EPSILON = 1e-05
ROPE_BASE = 10000.0
MASKED = -1e30
BF = jnp.bfloat16
F32 = jnp.float32
MIB = 1024 * 1024


def swap(values, axis, bit=1):
    count = lax.axis_size(axis)
    return lax.ppermute(values, axis, [(i, i ^ bit) for i in range(count)])


def fetch(values, offset):
    count = lax.axis_size("expert")
    return lax.ppermute(values, "expert", [(i, (i - offset) % count) for i in range(count)])


def deliver(values, offset):
    count = lax.axis_size("expert")
    return lax.ppermute(values, "expert", [(i, (i + offset) % count) for i in range(count)])


def halve(parts, bit_axis, bit):
    pairs = parts.reshape((parts.shape[0] // 2, 2) + parts.shape[1:])
    own = (lax.axis_index(bit_axis) // bit) % 2
    keep = lax.dynamic_index_in_dim(pairs, own, 1, keepdims=False)
    send = lax.dynamic_index_in_dim(pairs, 1 - own, 1, keepdims=False)
    got = swap(send, bit_axis, bit)
    return keep.astype(F32) + got.astype(F32)


def sum_over_dp(parts):
    bit = 1
    while parts.shape[0] > 1:
        parts = halve(parts.astype(BF), "dp", bit)
        bit *= 2
    return parts[0]


def exchange(parts):
    return lax.all_to_all(parts, "expert", split_axis=0, concat_axis=0, tiled=True)


def nn(left, right):
    return jnp.dot(left, right, preferred_element_type=F32)


def nt(left, right):
    return lax.dot_general(left, right, (((1,), (1,)), ((), ())), preferred_element_type=F32)


def tn(left, right):
    return lax.dot_general(left, right, (((0,), (0,)), ((), ())), preferred_element_type=F32)


def params(mib=60):
    return pltpu.CompilerParams(vmem_limit_bytes=mib * MIB)


def cost(micros):
    return pl.CostEstimate(flops=int(micros * 1e3), bytes_accessed=0, transcendentals=0)


def shaped(kind, *dims):
    return jax.ShapeDtypeStruct(dims, kind)


def full(*shape):
    return pl.BlockSpec(shape, lambda *_: (0,) * len(shape))


def after(values, *others):
    return lax.optimization_barrier((values,) + others)[0]


def turned(values, cosine, sine):
    lane = lax.broadcasted_iota(jnp.int32, values.shape, 1)
    quarter = HEAD_DIM // 2
    later = pltpu.roll(values, 2 * HEAD_DIM - quarter, 1)
    earlier = pltpu.roll(values, quarter, 1)
    return values * cosine + jnp.where(lane % HEAD_DIM < quarter, later, earlier) * sine


def project_kernel(x_ref, gain_ref, wq_ref, wk_ref, wv_ref, cos_ref, sin_ref, n_ref, q_ref, kv_ref, s_ref):
    values = x_ref[...].astype(F32)
    scale = lax.rsqrt(jnp.mean(values * values, axis=1, keepdims=True) + EPSILON)
    s_ref[...] = scale
    normed = (values * scale * gain_ref[...]).astype(BF)
    n_ref[...] = normed
    cosine, sine = cos_ref[...], sin_ref[...]
    lanes = 2 * HEAD_DIM
    kv = wk_ref.shape[1]
    keys = nn(normed, wk_ref[...])
    for i in range(0, kv, lanes):
        kv_ref[:, i : i + lanes] = turned(keys[:, i : i + lanes], cosine, sine).astype(BF)
    kv_ref[:, kv:] = nn(normed, wv_ref[...]).astype(BF)
    query = nn(normed, wq_ref[...])
    for i in range(0, query.shape[1], lanes):
        q_ref[:, i : i + lanes] = turned(query[:, i : i + lanes], cosine, sine).astype(BF)


def attend_kernel(groups, blocks, *refs):
    q_ref, kv_refs, bias_ref = refs[0], refs[1 : 1 + blocks], refs[1 + blocks]
    o_ref, low_ref, lse_ref, kv_ref = refs[2 + blocks :]
    h = HEAD_DIM
    rows = kv_refs[0].shape[0]
    for k in range(blocks):
        kv_ref[k * rows : (k + 1) * rows, :] = kv_refs[k][...]
    heads = kv_ref.shape[1] // (2 * h)
    for kv in range(heads):
        key = kv_ref[:, kv * h : kv * h + h]
        value = kv_ref[:, (heads + kv) * h : (heads + kv) * h + h]
        for g in range(groups):
            head = kv * groups + g
            span = slice(head * h, head * h + h)
            scores = nt(q_ref[:, span] * h**-0.5, key) + bias_ref[...]
            peak = jnp.max(scores, axis=1, keepdims=True)
            raw = jnp.exp(scores - peak)
            total = jnp.sum(raw, axis=1, keepdims=True)
            out = nn((raw * (1.0 / total)).astype(BF), value)
            o_ref[:, span] = out
            low_ref[:, span] = out.astype(BF)
            lse_ref[:, head : head + 1] = peak + jnp.log(total)


def attend_grad_kernel(groups, blocks, place_ref, *refs):
    q_ref, kv_refs, d_ref, o_ref, lse_ref, bias_ref = refs[0], refs[1 : 1 + blocks], *refs[1 + blocks : 5 + blocks]
    dq_ref, dkv_ref, kv_ref = refs[5 + blocks :]
    h = HEAD_DIM
    rows = kv_refs[0].shape[0]
    for k in range(blocks):
        kv_ref[k * rows : (k + 1) * rows, :] = kv_refs[k][...]
    heads = kv_ref.shape[1] // (2 * h)
    for kv in range(heads):
        key = kv_ref[:, kv * h : kv * h + h]
        value = kv_ref[:, (heads + kv) * h : (heads + kv) * h + h]
        key_grad = value_grad = None
        for g in range(groups):
            head = kv * groups + g
            span = slice(head * h, head * h + h)
            query = q_ref[:, span] * h**-0.5
            cot = d_ref[:, span]
            scores = nt(query, key) + bias_ref[...]
            probs = jnp.exp(scores - lse_ref[:, head : head + 1])
            delta = jnp.sum(cot.astype(F32) * o_ref[:, span], axis=1, keepdims=True)
            slope = (probs * (nt(cot, value) - delta)).astype(BF)
            value_part = tn(cot, probs.astype(BF))
            key_part = tn(query, slope)
            dq_ref[:, span] = nn(slope, key) * h**-0.5
            value_grad = value_part if value_grad is None else value_grad + value_part
            key_grad = key_part if key_grad is None else key_grad + key_part
        key_low = key_grad.astype(BF)
        value_low = value_grad.astype(BF)
        for k in range(blocks):
            to = lax.rem(place_ref[0] + k, blocks)
            dkv_ref[to, kv * h : kv * h + h, :] = key_low[:, k * rows : (k + 1) * rows]
            dkv_ref[to, (heads + kv) * h : (heads + kv) * h + h, :] = value_low[:, k * rows : (k + 1) * rows]


def middle_kernel(
    side_ref, x_ref, mine_ref, other_ref, w_ref, w_near, w_far, gain_ref, h_ref, s_ref, n_ref, own_ref, far_ref
):
    part = w_near.shape[0]
    hidden = x_ref[...].astype(F32) + nn(mine_ref[...], w_ref[...])
    for w, number in ((w_near, side_ref[1]), (w_far, 1 - side_ref[1])):
        hidden += nn(other_ref[:, pl.ds(pl.multiple_of(number * part, part), part)], w[...])
    h_ref[...] = hidden
    scale = lax.rsqrt(jnp.mean(hidden * hidden, axis=1, keepdims=True) + EPSILON)
    s_ref[...] = scale
    n_ref[...] = (hidden * scale * gain_ref[...]).astype(BF)
    half = own_ref.shape[0]
    own_ref[...] = n_ref[pl.ds(pl.multiple_of(side_ref[0] * half, half), half), :]
    far_ref[...] = n_ref[pl.ds(pl.multiple_of((1 - side_ref[0]) * half, half), half), :]


def make_pick(slot_ref, k, expert, slots):
    row = slot_ref[k, pl.ds(expert, 1), :]
    lines = lax.broadcasted_iota(jnp.int32, (slots, row.shape[1]), 0)
    return jnp.where(lines == row, 1.0, 0.0)


def cotangent_kernel(blocks, slots, *refs):
    slot_ref, halves, wd_ref = refs[0], refs[1 : 1 + 2 * blocks], refs[1 + 2 * blocks]
    cg_ref, dm_ref, x_ref = refs[2 + 2 * blocks :]
    half = x_ref.shape[1] // 2
    step = pl.program_id(0)

    @pl.when(step == 0)
    def _():
        for k in range(blocks):
            x_ref[k, :half, :] = halves[2 * k][:half, :]
            x_ref[k, half:, :] = halves[2 * k + 1][:half, :]

    for k in range(blocks):
        pick = make_pick(slot_ref, k, step, slots).astype(BF)
        cg_ref[0, k * slots : (k + 1) * slots, :] = nn(pick, x_ref[k]).astype(BF)
    dm_ref[0] = nt(cg_ref[0], wd_ref[0])


def split_rows(values):
    line = lax.broadcasted_iota(jnp.int32, (16, values[0].shape[1]), 0)
    out = jnp.zeros(line.shape, F32)
    for i, value in enumerate(values):
        high = value.astype(BF).astype(F32)
        out = jnp.where(line == 2 * i, high, jnp.where(line == 2 * i + 1, value - high, out))
    return out.astype(BF)


def pair_sum_kernel(mine_ref, got_ref, *outs):
    half = mine_ref.shape[1] - 16
    for k, out in enumerate(outs):
        total = mine_ref[k].astype(F32) + got_ref[k].astype(F32)
        out[:half, :] = total[:half].astype(BF)
        out[half:, :] = split_rows([total[half : half + 1] + total[half + 1 : half + 2]])


def gather_sum_kernel(*refs):
    parts, out = refs[:-1], refs[-1]
    half = out.shape[0] - 16
    total = parts[0][...].astype(F32)
    rows = [total[half : half + 1] + total[half + 1 : half + 2]]
    total = total[:half]
    for part in parts[1:]:
        more = part[...].astype(F32)
        total = total + more[:half]
        rows.append(more[half : half + 1] + more[half + 1 : half + 2])
    out[:half, :] = total.astype(BF)
    out[half:, :] = split_rows(rows)


def experts_kernel(blocks, slots, place_ref, slot_ref, *refs):
    halves, (hot_ref, router_ref, dm_ref, wg_ref, wu_ref) = refs[: 2 * blocks], refs[2 * blocks : 5 + 2 * blocks]
    (xg_ref, gm_ref, da_ref, db_ref, mine_ref, else_ref,
     x_ref, gates_ref, n_ref, pick_ref, dg_ref) = refs[5 + 2 * blocks :]
    rows = x_ref.shape[1]
    half = rows // 2
    step, steps = pl.program_id(0), pl.num_programs(0)

    @pl.when(step == 0)
    def _():
        for k in range(blocks):
            x_ref[k, :half, :] = halves[2 * k][...]
            x_ref[k, half:, :] = halves[2 * k + 1][...]
        tokens = x_ref[...].reshape(blocks * rows, x_ref.shape[2])
        hot = hot_ref[...] > 0.0
        logits = jnp.where(hot, nt(router_ref[...], tokens), MASKED)
        raw = jnp.where(hot, jnp.exp(logits - jnp.max(logits, axis=0, keepdims=True)), 0.0)
        gates_ref[...] = raw / jnp.sum(raw, axis=0, keepdims=True)
        dg_ref[...] = jnp.zeros_like(dg_ref)

    gate_row = gates_ref[pl.ds(place_ref[0] * steps + step, 1), :]
    at = pl.multiple_of(step * slots, slots)
    gate_parts, picks = [], []
    for k in range(blocks):
        pick = make_pick(slot_ref, k, step, slots)
        picks.append(pick)
        low = pick.astype(BF)
        pick_ref[k, pl.ds(at, slots), :] = low
        xg_ref[0, k * slots : (k + 1) * slots, :] = nn(low, x_ref[k]).astype(BF)
        gate_parts.append(jnp.sum(pick * gate_row[:, k * rows : (k + 1) * rows], axis=1, keepdims=True))
    gates = jnp.concatenate(gate_parts, axis=0)
    own = xg_ref[0]
    gate_pre = nn(own, wg_ref[0])
    up_pre = nn(own, wu_ref[0])
    raw_grad = dm_ref[0]
    sigmoid = 1.0 / (1.0 + jnp.exp(-gate_pre))
    swish = gate_pre * sigmoid
    active = swish * up_pre
    dgate = jnp.sum(active * raw_grad, axis=1, keepdims=True)
    gm_ref[0] = (gates * active).astype(BF)
    grad = gates * raw_grad
    da = (grad * up_pre * sigmoid * (1.0 + gate_pre * (1.0 - sigmoid))).astype(BF)
    db = (grad * swish).astype(BF)
    da_ref[0] = da
    db_ref[0] = db
    low = (nt(da, wg_ref[0]) + nt(db, wu_ref[0])).astype(BF)
    for k in range(blocks):
        part = slice(k * slots, (k + 1) * slots)
        n_ref[k, pl.ds(at, slots), :] = low[part]
        dg_row = jnp.sum(picks[k] * dgate[part], axis=0, keepdims=True)
        lanes = pl.ds(pl.multiple_of(step * half, half), half)
        dg_ref[2 * k : 2 * k + 1, lanes] = dg_row[:, :half]
        dg_ref[2 * k + 1 : 2 * k + 2, lanes] = dg_row[:, half:]

    @pl.when(step == steps - 1)
    def _():
        for k in range(blocks):
            out = tn(pick_ref[k], n_ref[k]).astype(BF)
            mine_ref[k, :half, :] = out[:half]
            else_ref[k, :half, :] = out[half:]
            mine_ref[k, half:, :] = split_rows([dg_ref[2 * k : 2 * k + 1, :]])
            else_ref[k, half:, :] = split_rows([dg_ref[2 * k + 1 : 2 * k + 2, :]])


def weights_kernel(own_ref, cg_ref, *refs):
    pairs, outs = refs[:8], refs[8:]
    count, width = len(outs) * outs[0].shape[0], outs[0].shape[3]
    split = pairs[0].shape[1]
    for number in range(count):
        if len(outs) == 1:
            out, place, span = outs[0], number, slice(number * width, (number + 1) * width)
        else:
            out, place = outs[number % 2], number // 2
            span = pl.ds(pl.multiple_of((own_ref[0] ^ number) * width, 128), width)
        gate = up = down = None
        for i in range(2):
            xg_ref, gm_ref, da_ref, db_ref = pairs[4 * i : 4 * i + 4]
            rows = xg_ref[0, :, span]
            cots = cg_ref[0, i * split : (i + 1) * split, span]
            parts = tn(rows, da_ref[0]), tn(rows, db_ref[0]), tn(cots, gm_ref[0])
            gate, up, down = parts if i == 0 else (gate + parts[0], up + parts[1], down + parts[2])
        out[place, 0, 0] = gate.astype(BF)
        out[place, 0, 1] = up.astype(BF)
        out[place, 0, 2] = down.astype(BF)


def finish_kernel(parts, *refs):
    gate_ref, up_ref, down_ref = refs[-3:]
    total = None
    for ref in refs[:parts]:
        term = ref[(0,) * (len(ref.shape) - 3)].astype(F32)
        total = term if total is None else total + term
    gate_ref[0] = total[0]
    up_ref[0] = total[1]
    down_ref[0] = total[2].T


def combine_kernel(slots, offsets, where_ref, slot_ref, ga_ref, gb_ref, wd_ref, mine_ref, else_ref, r_ref, pick_ref):
    blocks = mine_ref.shape[0]
    group = blocks // 2
    step, steps = pl.program_id(0), pl.num_programs(0)
    at = pl.multiple_of(step * slots, slots)
    for i, ref in enumerate((ga_ref, gb_ref)):
        low = nn(ref[0], wd_ref[0]).astype(BF)
        for j in range(group):
            k = i * group + j
            r_ref[k, pl.ds(at, slots), :] = low[j * slots : (j + 1) * slots]
            pick_ref[k, pl.ds(at, slots), :] = make_pick(slot_ref, k, step, slots).astype(BF)

    @pl.when(step == steps - 1)
    def _():
        width = mine_ref.shape[2]
        half = mine_ref.shape[1] // 2
        own = pl.ds(pl.multiple_of(where_ref[0] * width, width), width)
        far = pl.ds(pl.multiple_of((1 - where_ref[0]) * width, width), width)
        for k in range(blocks):
            to = lax.rem(where_ref[1] + offsets[k], blocks)
            mine_ref[to] = tn(pick_ref[k], r_ref[k, :, own]).astype(BF)
            out = tn(pick_ref[k], r_ref[k, :, far]).astype(BF)
            else_ref[to, :half] = out[half:]
            else_ref[to, half:] = out[:half]


def norm_grad_kernel(
    local, top, where_ref, own_ref, far_ref, n_ref, chosen_ref, router_ref, h_ref, s_ref, gain_ref, c_ref, w_ref,
    grad_ref, low_ref, term_ref, do_ref, dl_ref, e_ref, g_ref,
):
    side, place = where_ref[0], where_ref[1]
    half = own_ref.shape[0] - 16
    lanes = router_ref.shape[1]
    sources = 4
    g_ref[...] = jnp.zeros_like(g_ref)
    for part, ref in ((side, own_ref), (1 - side, far_ref)):
        e_ref[pl.ds(pl.multiple_of(part * half, half), half), :] = ref[:half, :]
        tail = ref[half:, :].astype(F32)
        for k in range(sources):
            row = tail[2 * k : 2 * k + 1] + tail[2 * k + 1 : 2 * k + 2]
            source = lax.rem(place + sources - k, sources)
            for e in range(local):
                g_ref[part, pl.ds(source * local + e, 1), :] = row[:, e * half : (e + 1) * half]
    dgate = jnp.concatenate([g_ref[0].T, g_ref[1].T], axis=0)
    lane = lax.broadcasted_iota(jnp.int32, dgate.shape, 1)
    hot = chosen_ref[:, 0:1] == lane
    for i in range(1, top):
        hot = hot | (chosen_ref[:, i : i + 1] == lane)
    logits = jnp.where(hot, nn(n_ref[...], router_ref[...]), MASKED)
    raw = jnp.where(hot, jnp.exp(logits - jnp.max(logits, axis=1, keepdims=True)), 0.0)
    gates = raw / jnp.sum(raw, axis=1, keepdims=True)
    logit_grads = (gates * (dgate - jnp.sum(gates * dgate, axis=1, keepdims=True))).astype(BF)
    dl_ref[...] = logit_grads
    grad = nt(logit_grads, router_ref[...]) + e_ref[...].astype(F32)
    hidden, scale = h_ref[...], s_ref[...]
    term_ref[...] = (grad * hidden * scale).astype(BF)
    weighted = grad * gain_ref[...]
    inner = jnp.mean(weighted * hidden, axis=1, keepdims=True)
    total = scale * weighted - hidden * (scale * scale * scale) * inner + c_ref[...].astype(F32)
    grad_ref[...] = total
    low = total.astype(BF)
    low_ref[...] = low
    do_ref[...] = nt(low, w_ref[...]).astype(BF)


def place_direct(own, blocks_z, scratch, keep_ref, send_ref):
    blocks, rows, _ = keep_ref.shape
    core = lax.rem(own, 2)
    for out, bit in ((keep_ref, core), (send_ref, 1 - core)):
        for number in range(blocks):
            at = ((2 * (number // blocks_z) + bit) * blocks_z + number % blocks_z) * rows
            out[number] = scratch[pl.ds(pl.multiple_of(at, 8), rows), :].astype(BF)


def place_slices(own, scratch, keep_ref, send_ref):
    blocks, pairs, rows, _ = keep_ref.shape
    for a in range(2 * pairs):
        out = send_ref if a % 2 else keep_ref
        for b in range(blocks):
            number = (own ^ a) * blocks + b
            out[b, a // 2] = scratch[pl.ds(pl.multiple_of(number * rows, 8), rows), :].astype(BF)


def early_kernel(
    where_ref, low_ref, o_ref, n_ref, dl_ref, term_ref, first_ref, dq_ref, cos_ref, sin_ref,
    keep_ref, send_ref, turned_ref, scratch,
):
    width, lanes = o_ref.shape[1], 2 * HEAD_DIM
    tail = dl_ref.shape[1]
    for i in range(0, width, lanes):
        turned_ref[:, i : i + lanes] = turned(dq_ref[:, i : i + lanes], cos_ref[...], -sin_ref[...]).astype(BF)
    scratch[:, :width] = tn(low_ref[...], o_ref[...])
    lane = lax.broadcasted_iota(jnp.int32, dl_ref.shape, 1)
    ones = jnp.where(lane == tail - 1, 1.0, 0.0).astype(BF)
    scratch[:, width : width + tail] = tn(n_ref[...], dl_ref[...]) + tn(term_ref[...], ones)
    scratch[:, width + tail :] = tn(first_ref[...], turned_ref[...])
    place_slices(where_ref[0], scratch, keep_ref, send_ref)


def input_kernel(dq_ref, kv_ref, cos_ref, sin_ref, wq_ref, wk_ref, wv_ref, x_ref, s_ref,
                 grads_ref, part_ref, term_ref):
    lanes = 2 * HEAD_DIM
    kv_width = wk_ref.shape[1]
    total = jnp.sum(kv_ref[...].astype(F32), axis=0).T
    for i in range(0, kv_width, lanes):
        grads_ref[:, i : i + lanes] = turned(total[:, i : i + lanes], cos_ref[...], -sin_ref[...]).astype(BF)
    grads_ref[:, kv_width:] = total[:, kv_width:].astype(BF)
    part = (
        nt(dq_ref[...], wq_ref[...])
        + nt(grads_ref[:, :kv_width], wk_ref[...])
        + nt(grads_ref[:, kv_width:], wv_ref[...])
    )
    part_ref[...] = part.astype(BF)
    term = jnp.sum(part * x_ref[...].astype(F32) * s_ref[...], axis=0, keepdims=True)
    line = lax.broadcasted_iota(jnp.int32, term_ref.shape, 0)
    term_ref[...] = jnp.where(line == 0, term, 0.0)


def late_kernel(blocks_z, where_ref, n_ref, grads_ref, term_ref, other_ref, keep_ref, send_ref, scratch):
    width = grads_ref.shape[1]
    scratch[:, :width] = tn(n_ref[...], grads_ref[...])
    ones = jnp.ones((term_ref.shape[0], scratch.shape[1] - width), BF)
    scratch[:, width:] = tn((term_ref[...] + other_ref[...]).astype(BF), ones)
    place_direct(where_ref[0], blocks_z, scratch, keep_ref, send_ref)


def near_sum(keep, send):
    return keep.astype(F32) + swap(send, "dp", 1).astype(F32)


def place_sum(total):
    return jnp.sum(exchange(total.astype(BF)).astype(F32), axis=0)


def far_sum(total, axis):
    bit = 1
    while total.shape[axis] > 1:
        bit *= 2
        lead = total.shape[:axis]
        pairs = total.reshape(lead + (total.shape[axis] // 2, 2) + total.shape[axis + 1 :])
        keep = lax.index_in_dim(pairs, 0, axis + 1, keepdims=False)
        send = lax.index_in_dim(pairs, 1, axis + 1, keepdims=False)
        total = keep + swap(send.astype(BF), "dp", bit).astype(F32)
    return jnp.squeeze(total, axis)


def norm_backward(values, norm_scale, gain, grad_normed):
    weighted = grad_normed * gain
    inner = jnp.mean(weighted * values, axis=1, keepdims=True)
    grad_values = norm_scale * weighted - values * (norm_scale * norm_scale * norm_scale) * inner
    grad_gain = jnp.sum(grad_normed * values * norm_scale, axis=0)
    return (grad_values, grad_gain)


def rotary_tables(length):
    half = HEAD_DIM // 2
    inverse = ROPE_BASE ** (-2.0 * np.arange(half) / HEAD_DIM)
    angles = np.arange(length)[:, None] * inverse[None, :]
    cosine, sine = np.cos(angles), np.sin(angles)
    return (
        np.concatenate([cosine, cosine, cosine, cosine], axis=1).astype(np.float32),
        np.concatenate([-sine, sine, -sine, sine], axis=1).astype(np.float32),
    )


def body(
    x_in,
    segments,
    chosen,
    out_grad,
    norm1_gain,
    w_query,
    w_key,
    w_value,
    w_out,
    norm2_gain,
    w_router,
    w_gate,
    w_up,
    w_down,
):
    tok_rows, full_width = x_in.shape
    h = HEAD_DIM
    q_width, kv_width = w_query.shape[1], w_key.shape[1]
    groups = q_width // kv_width
    experts_local, _, inner = w_gate.shape
    n_exp, n_dp = lax.axis_size("expert"), lax.axis_size("dp")
    total_experts = experts_local * n_exp
    top_count = chosen.shape[1]
    capacity = tok_rows * top_count * 25 // (16 * total_experts)
    place, side = lax.axis_index("expert"), lax.axis_index("tensor")
    half_width = full_width // lax.axis_size("tensor")
    row_start = place * tok_rows
    seq_length = segments.shape[0]
    half_rows = tok_rows // 2

    own_dp = lax.axis_index("dp")
    order = [1, 3, 2, 0] if n_exp == 4 else [*range(1, n_exp), 0]
    group = n_exp // 2
    vmem = lambda *shape: pltpu.VMEM(shape, BF)
    prefetch = pltpu.PrefetchScalarGridSpec

    tables = [
        lax.dynamic_slice_in_dim(jnp.asarray(table), row_start, tok_rows)
        for table in rotary_tables(seq_length)
    ]
    cosine, sine = tables
    normed_one, query_rot, kv_own, scale_one = pl.pallas_call(
        project_kernel,
        name="project",
        out_shape=(
            shaped(BF, tok_rows, full_width),
            shaped(BF, tok_rows, q_width),
            shaped(BF, tok_rows, 2 * kv_width),
            shaped(F32, tok_rows, 1),
        ),
        compiler_params=params(),
        cost_estimate=cost(2),
    )(x_in, norm1_gain[None], w_query, w_key, w_value, cosine, sine)
    kv_blocks = [kv_own] + [fetch(kv_own, k) for k in range(1, n_exp)]

    turned_segments = lax.dynamic_slice_in_dim(
        jnp.concatenate([segments, segments]), row_start, seq_length
    )
    key_positions = (row_start + jnp.arange(seq_length, dtype=jnp.int32)) % seq_length
    allowed = (turned_segments[:tok_rows, None] == turned_segments[None, :]) & (
        key_positions[:tok_rows, None] >= key_positions[None, :]
    )
    bias = jnp.where(allowed, 0.0, MASKED).astype(F32)
    heads = q_width // h
    out_half = w_out.shape[0] // 2
    own_core = own_dp % 2
    w_near = swap(lax.dynamic_slice_in_dim(w_out, own_core * out_half, out_half), "tensor")
    w_far = swap(w_near, "dp", 1)
    tail_lanes = -(-(total_experts + 1) // 128) * 128
    router_wide = jnp.pad(w_router, ((0, 0), (0, tail_lanes - total_experts)))
    chosen_wide = jnp.pad(chosen, ((0, 0), (0, 128 - top_count)))
    query_rot, router_wide, chosen_wide = lax.optimization_barrier((query_rot, router_wide, chosen_wide))
    attended, attended_low, log_totals = pl.pallas_call(
        functools.partial(attend_kernel, groups, n_exp),
        name="attend",
        out_shape=(
            shaped(F32, tok_rows, q_width),
            shaped(BF, tok_rows, q_width),
            shaped(F32, tok_rows, heads),
        ),
        scratch_shapes=[vmem(seq_length, 2 * kv_width)],
        compiler_params=params(),
        cost_estimate=cost(10),
    )(after(query_rot, w_near), *kv_blocks, bias)

    cot_in, chosen_in = out_grad, chosen
    cot_half = lambda s: lax.dynamic_slice_in_dim(cot_in, s * half_rows, half_rows)
    chosen_half = lambda s: jnp.pad(
        lax.dynamic_slice_in_dim(chosen_in, s * half_rows, half_rows).T.astype(BF),
        ((0, 16 - top_count), (0, full_width - half_rows)),
    )
    payload = lambda s: jnp.concatenate([cot_half(s), chosen_half(s)], axis=0)
    cot_own, cot_other = payload(side), payload(1 - side)
    cot_near = {}
    for k in order:
        cot_near[k] = fetch(after(cot_own, *kv_blocks[1:]), k) if k else cot_own
    expert_slots = n_exp * capacity
    by_expert = lambda *tail: pl.BlockSpec((1,) + tail, lambda e, *_: (e,) + (0,) * len(tail))

    middle_in = (x_in, attended_low, swap(attended_low, "tensor"), w_out, w_near, w_far, norm2_gain[None])
    whole = lambda array: full(*array.shape)
    hidden_one, scale_two, normed_two, normed_own, normed_far = pl.pallas_call(
        middle_kernel,
        name="middle",
        grid_spec=prefetch(
            num_scalar_prefetch=1,
            grid=(1,),
            in_specs=[whole(array) for array in middle_in],
            out_specs=(
                full(tok_rows, full_width),
                full(tok_rows, 1),
                full(tok_rows, full_width),
                full(half_rows, full_width),
                full(half_rows, full_width),
            ),
        ),
        out_shape=(
            shaped(F32, tok_rows, full_width),
            shaped(F32, tok_rows, 1),
            shaped(BF, tok_rows, full_width),
            shaped(BF, half_rows, full_width),
            shaped(BF, half_rows, full_width),
        ),
        compiler_params=params(24),
        cost_estimate=cost(2),
    )(jnp.stack([side, own_core]), *middle_in)
    near_rows = {k: fetch(normed_own, k) for k in order[:group]}
    for k in order[group:]:
        near_rows[k] = fetch(after(normed_own, *near_rows.values()), k) if k else normed_own

    cot_pairs = [
        (cot_near[k], swap(after(cot_near[k], normed_own), "tensor") if k else cot_other)
        for k in order
    ]
    chosen_blocks = jnp.stack(
        [
            jnp.concatenate([part[half_rows : half_rows + top_count, :half_rows] for part in pair], axis=1)
            for pair in cot_pairs
        ]
    ).astype(jnp.int32)
    expert_ids = jnp.arange(total_experts, dtype=jnp.int32)
    hot_all = jnp.any(chosen_blocks[:, :, None, :] == expert_ids[:, None], axis=1)
    hot_rows = hot_all.transpose(1, 0, 2).reshape(total_experts, n_exp * tok_rows).astype(F32)
    hot_local = lax.dynamic_slice_in_dim(hot_all, place * experts_local, experts_local, 1)
    token_row = jnp.arange(tok_rows, dtype=jnp.int32)
    before = (token_row[:, None] < token_row[None, :]).astype(BF)
    rank = jnp.einsum("kes,st->ket", hot_local.astype(BF), before, preferred_element_type=F32)
    slot_of = jnp.where(hot_local, rank.astype(jnp.int32), -1)

    cot_slots, raw_grad = pl.pallas_call(
        functools.partial(cotangent_kernel, n_exp, capacity),
        name="cotangent",
        grid=(experts_local,),
        in_specs=[whole(slot_of)]
        + [full(*cot_own.shape)] * (2 * n_exp)
        + [by_expert(inner, full_width)],
        out_specs=(by_expert(expert_slots, full_width), by_expert(expert_slots, inner)),
        out_shape=(
            shaped(BF, experts_local, expert_slots, full_width),
            shaped(F32, experts_local, expert_slots, inner),
        ),
        scratch_shapes=[vmem(n_exp, tok_rows, full_width)],
        compiler_params=params(),
        cost_estimate=cost(13),
    )(slot_of, *[half for pair in cot_pairs for half in pair], w_down)

    far_rows = {
        k: swap(near_rows[k], "tensor") if k else normed_far for k in order
    }

    def run_experts(number, hold):
        ks = order[number * group : (number + 1) * group]
        token_halves = [half for k in ks for half in (near_rows[k], far_rows[k])]
        token_halves[0] = after(token_halves[0], *hold)
        slots_here = group * capacity
        low_slots = shaped(BF, experts_local, slots_here, inner)
        columns = group * tok_rows
        return pl.pallas_call(
            functools.partial(experts_kernel, group, capacity),
            name="experts",
            grid_spec=prefetch(
                num_scalar_prefetch=1,
                grid=(experts_local,),
                in_specs=[full(group, experts_local, tok_rows)]
                + [full(half_rows, full_width)] * (2 * group)
                + [
                    pl.BlockSpec((total_experts, columns), lambda e, *_: (0, number)),
                    full(total_experts, full_width),
                    pl.BlockSpec((1, slots_here, inner), lambda e, *_: (e, number, 0)),
                    by_expert(full_width, inner),
                    by_expert(full_width, inner),
                ],
                out_specs=(
                    by_expert(slots_here, full_width),
                    by_expert(slots_here, inner),
                    by_expert(slots_here, inner),
                    by_expert(slots_here, inner),
                    full(group, half_rows + 16, full_width),
                    full(group, half_rows + 16, full_width),
                ),
                scratch_shapes=[
                    vmem(group, tok_rows, full_width),
                    pltpu.VMEM((total_experts, columns), F32),
                    vmem(group, experts_local * capacity, full_width),
                    vmem(group, experts_local * capacity, tok_rows),
                    pltpu.VMEM((2 * group, full_width), F32),
                ],
            ),
            out_shape=(
                shaped(BF, experts_local, slots_here, full_width),
                low_slots,
                low_slots,
                low_slots,
                shaped(BF, group, half_rows + 16, full_width),
                shaped(BF, group, half_rows + 16, full_width),
            ),
            compiler_params=params(),
            cost_estimate=cost(18),
        )(
            place[None], slot_of[number * group : (number + 1) * group], *token_halves,
            hot_rows, w_router.T, raw_grad, w_gate, w_up,
        )

    first = run_experts(0, [far_rows[k] for k in order[group:]])
    second = run_experts(1, [first[4]])

    def pair_sum(made, got):
        return pl.pallas_call(
            pair_sum_kernel,
            name="pair_sum",
            out_shape=(shaped(BF, half_rows + 16, full_width),) * group,
            compiler_params=params(24),
            cost_estimate=cost(1),
        )(made[4], got)

    first_sums = pair_sum(first, swap(first[5], "tensor"))
    second_got = swap(second[5], "tensor")

    out_dims = (n_exp, tok_rows, half_width)

    def combine(*hold):
        return pl.pallas_call(
            functools.partial(combine_kernel, capacity, order),
            name="combine",
            grid_spec=prefetch(
                num_scalar_prefetch=1,
                grid=(experts_local,),
                in_specs=[
                    whole(slot_of),
                    by_expert(group * capacity, inner),
                    by_expert(group * capacity, inner),
                    by_expert(inner, full_width),
                ],
                out_specs=(full(*out_dims), full(*out_dims)),
                scratch_shapes=[
                    vmem(n_exp, experts_local * capacity, full_width),
                    vmem(n_exp, experts_local * capacity, tok_rows),
                ],
            ),
            out_shape=(shaped(BF, *out_dims), shaped(BF, *out_dims)),
            compiler_params=params(),
            cost_estimate=cost(12),
        )(after(jnp.stack([side, place]), *hold), slot_of, first[1], second[1], w_down)

    slice_width = full_width // n_dp
    pairs = [*first[:4], *second[:4]]
    crossing = 1 if n_dp == 4 and experts_local > 3 and slice_width % 128 == 0 else 0
    summed = experts_local - crossing

    def weights(base, count, outs, *hold):
        some = lambda *tail: pl.BlockSpec((1,) + tail, lambda e, *_: (base + e,) + (0,) * len(tail))
        shape = (n_dp // outs, count, 3, slice_width, inner)
        return pl.pallas_call(
            weights_kernel,
            name="weights",
            grid_spec=prefetch(
                num_scalar_prefetch=1,
                grid=(count,),
                in_specs=[some(expert_slots, full_width)] + [some(*array.shape[1:]) for array in pairs],
                out_specs=(pl.BlockSpec((shape[0], 1) + shape[2:], lambda e, *_: (0, e, 0, 0, 0)),) * outs,
            ),
            out_shape=(shaped(BF, *shape),) * outs,
            compiler_params=params(),
            cost_estimate=cost(12),
        )(after(own_dp[None], *hold), cot_slots, *pairs)

    early_experts = summed // 4
    out_mine, out_else = combine(*first_sums, second[4])
    first_grads = weights(0, early_experts, 1, out_mine)[0]
    terms = {k: deliver(first_sums[i], k) for i, k in enumerate(order[:group])}
    second_got, *arrived = lax.optimization_barrier((second_got, first_grads, *terms.values()))
    terms = dict(zip(terms, arrived[1:]))
    second_sums = pair_sum(second, second_got)
    for i, k in enumerate(order[group:]):
        terms[k] = deliver(second_sums[i], k) if k else second_sums[i]
    out_got = swap(after(out_else, second_sums[0]), "tensor")
    out_low = (out_mine.astype(F32) + out_got.astype(F32)).astype(BF)

    first_sum = lax.psum_scatter(
        after(first_grads, *second_sums), "dp", scatter_dimension=0, tiled=False
    )
    weight_grads = weights(early_experts, summed - early_experts, 1, *second_sums)[0]
    keep, send = weights(summed, crossing, 2, weight_grads) if crossing else (second_sums[0],) * 2
    half_sum = pl.pallas_call(
        gather_sum_kernel,
        name="gather_sum",
        out_shape=shaped(BF, half_rows + 16, full_width),
        compiler_params=params(24),
        cost_estimate=cost(1),
    )(after(terms[0], weight_grads, keep, out_low), *[terms[k] for k in range(1, n_exp)])
    weight_sum = lax.psum_scatter(
        after(weight_grads, half_sum), "dp", scatter_dimension=0, tiled=False
    )
    half_other = swap(half_sum, "tensor")
    if crossing:
        near = swap(after(send, half_other), "dp", 1)
        half_grads = (keep[1].astype(F32) + near[1].astype(F32)).astype(BF)
    out_home = exchange(after(out_low, half_sum))

    back_in = (
        half_sum, half_other, normed_two, chosen_wide, router_wide, hidden_one, scale_two, norm2_gain[None], out_grad, w_out,
    )
    hidden_grad, branch_cot, gain_two_term, attended_grad, logit_grads = pl.pallas_call(
        functools.partial(norm_grad_kernel, experts_local, top_count),
        name="norm_grad",
        grid_spec=prefetch(
            num_scalar_prefetch=1,
            grid=(1,),
            in_specs=[whole(array) for array in back_in],
            out_specs=(
                full(tok_rows, full_width),
                full(tok_rows, full_width),
                full(tok_rows, full_width),
                full(tok_rows, q_width),
                full(tok_rows, tail_lanes),
            ),
            scratch_shapes=[vmem(tok_rows, full_width), pltpu.VMEM((2, tail_lanes, half_rows), F32)],
        ),
        out_shape=(
            shaped(F32, tok_rows, full_width),
            shaped(BF, tok_rows, full_width),
            shaped(BF, tok_rows, full_width),
            shaped(BF, tok_rows, q_width),
            shaped(BF, tok_rows, tail_lanes),
        ),
        compiler_params=params(),
        cost_estimate=cost(4),
    )(jnp.stack([side, place]), *back_in)

    back_args = (query_rot, *kv_blocks, attended_grad, attended, log_totals, bias)
    query_grads, kv_parts = pl.pallas_call(
        functools.partial(attend_grad_kernel, groups, n_exp),
        name="attend_grad",
        grid_spec=prefetch(
            num_scalar_prefetch=1,
            grid=(1,),
            in_specs=[whole(array) for array in back_args],
            out_specs=(full(tok_rows, q_width), full(n_exp, 2 * kv_width, tok_rows)),
            scratch_shapes=[vmem(seq_length, 2 * kv_width)],
        ),
        out_shape=(shaped(F32, tok_rows, q_width), shaped(BF, n_exp, 2 * kv_width, tok_rows)),
        compiler_params=params(),
        cost_estimate=cost(10),
    )(place[None], *back_args)
    kv_terms = exchange(after(kv_parts, out_home))

    slice_rows = full_width // (n_dp * n_exp)

    def slices_of(kernel, name, width, more, *arrays):
        dims = (n_exp, n_dp // 2, slice_rows, width)
        dims = dims if more else (n_exp * n_dp // 2, slice_rows, width)
        return pl.pallas_call(
            kernel,
            name=name,
            grid_spec=prefetch(
                num_scalar_prefetch=1,
                grid=(1,),
                in_specs=[whole(array) for array in arrays],
                out_specs=(full(*dims), full(*dims)) + tuple(full(*dim) for dim in more),
                scratch_shapes=[pltpu.VMEM((full_width, width), F32)],
            ),
            out_shape=(shaped(BF, *dims), shaped(BF, *dims)) + tuple(shaped(BF, *dim) for dim in more),
            compiler_params=params(),
            cost_estimate=cost(5),
        )(own_dp[None], *arrays)

    early_keep, early_send, query_low = slices_of(
        early_kernel, "early", 2 * q_width + tail_lanes, [(tok_rows, q_width)],
        branch_cot, attended_low, normed_two, logit_grads, gain_two_term, normed_one, query_grads, cosine, sine,
    )
    early = near_sum(early_keep, early_send).astype(BF)
    if crossing:
        kv_terms, half_grads = lax.optimization_barrier((kv_terms, half_grads))
    kv_terms, early = lax.optimization_barrier((kv_terms, early))
    grads_low, partial_low, gain_one_term = pl.pallas_call(
        input_kernel,
        name="input",
        out_shape=(
            shaped(BF, tok_rows, 2 * kv_width),
            shaped(BF, tok_rows, full_width),
            shaped(F32, 16, full_width),
        ),
        compiler_params=params(),
        cost_estimate=cost(4),
    )(query_low, kv_terms, cosine, sine, w_query, w_key, w_value, x_in, scale_one)
    partial_other = swap(partial_low, "tensor")
    late_keep, late_send = slices_of(
        functools.partial(late_kernel, n_exp), "late", 2 * kv_width + 128, (), normed_one, grads_low, gain_one_term, swap(gain_one_term, "tensor")
    )
    late_send, partial_other = lax.optimization_barrier((late_send, partial_other))
    late = near_sum(late_keep, late_send).astype(BF)
    early = place_sum(early)
    late, partial_other, early = lax.optimization_barrier((late, partial_other, early))
    same_core = [
        [dp * n_exp + z for dp in range(core, n_dp, 2) for z in range(n_exp)] for core in range(2)
    ]
    late_parts = lax.all_to_all(
        late, ("dp", "expert"), split_axis=0, concat_axis=0, tiled=True, axis_index_groups=same_core
    )
    if crossing:
        far = swap(after(half_grads, early), "dp", 2)
    early = far_sum(early, 0)

    def finish(base, count, totals, specs, earlier):
        some = lambda *tail: pl.BlockSpec((1,) + tail, lambda e: (base + e,) + (0,) * len(tail))
        return pl.pallas_call(
            functools.partial(finish_kernel, len(totals)),
            name="finish",
            grid=(count,),
            in_specs=specs + [pl.BlockSpec(memory_space=pl.ANY)] * len(earlier),
            out_specs=(some(slice_width, inner), some(slice_width, inner), some(inner, slice_width)),
            out_shape=(
                shaped(F32, experts_local, slice_width, inner),
                shaped(F32, experts_local, slice_width, inner),
                shaped(F32, experts_local, inner, slice_width),
            ),
            input_output_aliases={len(totals) + i: i for i in range(len(earlier))},
            compiler_params=params(24),
            cost_estimate=cost(3),
        )(*totals, *earlier)

    one = by_expert(3, slice_width, inner)
    finals = finish(0, early_experts, (after(first_sum, partial_other),), [one], ())
    finals = finish(early_experts, summed - early_experts, (weight_sum,), [one], finals)
    if crossing:
        lead = pl.BlockSpec((1, 1, 3, slice_width, inner), lambda e: (0, e, 0, 0, 0))
        finals = finish(summed, crossing, (keep, near, far), [lead, lead, one], finals)
    grad_gate, grad_up, grad_down = finals
    late = jnp.sum(after(late_parts, grad_gate).astype(F32), axis=0)

    mixture_half = jnp.sum(out_home.astype(F32), axis=0)
    mixture_half = jnp.where(side == 0, mixture_half, jnp.roll(mixture_half, half_rows, axis=0))
    residual_half = lax.dynamic_slice_in_dim(hidden_one, side * half_width, half_width, 1)
    block_out = (residual_half + mixture_half).astype(BF)

    normed_one_grad = partial_low.astype(F32) + partial_other.astype(F32)
    inputs = x_in.astype(F32)
    input_part, _ = norm_backward(inputs, scale_one, norm1_gain, normed_one_grad)
    input_grad = hidden_grad + input_part
    gain_one = late[:, -1]
    return (
        block_out,
        input_grad,
        gain_one,
        early[:, q_width + tail_lanes :],
        late[:, :kv_width],
        late[:, kv_width : 2 * kv_width],
        early[:, :q_width].T,
        early[:, q_width + tail_lanes - 1],
        early[:, q_width : q_width + total_experts],
        grad_gate,
        grad_up,
        grad_down,
    )


def solution(mesh):
    return jax.shard_map(
        body,
        mesh=mesh,
        in_specs=(
            P(("dp", "expert"), None),
            P("dp"),
            P(("dp", "expert"), None),
            P(("dp", "expert"), None),
            P(),
            P(None, "tensor"),
            P(None, "tensor"),
            P(None, "tensor"),
            P("tensor", None),
            P(),
            P(),
            P("expert", None, "tensor"),
            P("expert", None, "tensor"),
            P("expert", "tensor", None),
        ),
        out_specs=(
            P(("dp", "expert"), "tensor"),
            P(("dp", "expert"), None),
            P(("dp", "expert")),
            P(("dp", "expert"), "tensor"),
            P(("dp", "expert"), "tensor"),
            P(("dp", "expert"), "tensor"),
            P("tensor", ("dp", "expert")),
            P(("dp", "expert")),
            P(("dp", "expert"), None),
            P("expert", "dp", "tensor"),
            P("expert", "dp", "tensor"),
            P("expert", "tensor", "dp"),
        ),
        check_vma=False,
    )
```

profile of v0, /device:TPU:0, one launch (start us, length us, event | category | flops | bytes accessed | tf_op | source)
XLA Modules:
  0.0 431.0 jit_solution(1669147746046092799)
XLA Ops:
  24.4 13.3 %collective-permute-done.w_near = bf16[384,1536]{1,0:T(8,128)(2,1)} collective-permute-done((bf16[384,1536]{1,0:T(8,128)(2,1)S(1)}, bf16[384,1536]{1,0:T(8,128)(2,1)}, u32[]{:S(2)}, u32[]{:S(2)}) %collective-permute-start) | collective-permute-done | bytes 1179680 | tf_op jit(solution)/shard_map/ppermute | solution.py:22
  40.0 6.1 %collective-permute-start.8 = (bf16[144,1536]{1,0:T(8,128)(2,1)}, bf16[144,1536]{1,0:T(8,128)(2,1)}, u32[]{:S(2)}, u32[]{:S(2)}) collective-permute-start(bf16[144,1536]{1,0:T(8,128)(2,1)} %fusion.13.refs_7_), channel_id=1, source_target_pairs={{0,2},{2,4},{4,6},{6,0},{1,3},{3,5},{5,7},{7,1},{8,10},{10,12},{12... | collective-permute-start | bytes 1327112 | tf_op jit(solution)/shard_map/ppermute | solution.py:27
  50.6 10.8 %attend.1 = (f32[256,768]{1,0:T(8,128)}, bf16[256,768]{1,0:T(8,128)(2,1)}, f32[256,12]{1,0:T(8,128)}) custom-call(bf16[256,768]{1,0:T(8,128)(2,1)} %get-tuple-element.109.refs_0_, bf16[256,512]{1,0:T(8,128)(2,1)} %get-tuple-element.110.refs_1_, bf16[256,512]{1,0:T(8,128)(2,1)} %copy-done.25, bf16[256,512]{1,0:T(8,128)(2,1)} %copy-done.24, ...), custom_call_target="tpu_custom_call" | custom-call | flops 10000 | tf_op jit(solution)/shard_map/attend/pallas_call | solution.py:578
  62.5 8.7 %collective-permute-done.4.other_ref = bf16[256,768]{1,0:T(8,128)(2,1)S(1)} collective-permute-done((bf16[256,768]{1,0:T(8,128)(2,1)}, bf16[256,768]{1,0:T(8,128)(2,1)S(1)}, u32[]{:S(2)}, u32[]{:S(2)}) %collective-permute-start.4) | collective-permute-done | bytes 393248 | tf_op jit(solution)/shard_map/ppermute | solution.py:22
  86.1 5.2 %collective-permute-done.10.refs_5_ = bf16[144,1536]{1,0:T(8,128)(2,1)} collective-permute-done((bf16[144,1536]{1,0:T(8,128)(2,1)}, bf16[144,1536]{1,0:T(8,128)(2,1)}, u32[]{:S(2)}, u32[]{:S(2)}) %collective-permute-start.10) | collective-permute-done | bytes 442400 | tf_op jit(solution)/shard_map/ppermute | solution.py:27
  96.2 5.5 %collective-permute-done.12.refs_0_ = bf16[128,1536]{1,0:T(8,128)(2,1)S(1)} collective-permute-done((bf16[128,1536]{1,0:T(8,128)(2,1)S(1)}, bf16[128,1536]{1,0:T(8,128)(2,1)S(1)}, u32[]{:S(2)}, u32[]{:S(2)}) %collective-permute-start.12) | collective-permute-done | bytes 393248 | tf_op jit(solution)/shard_map/ppermute | solution.py:27
  111.4 14.7 %cotangent.1 = (bf16[10,320,1536]{2,1,0:T(8,128)(2,1)}, f32[10,320,256]{2,1,0:T(8,128)}) custom-call(s32[4,10,256]{2,1,0:T(8,128)} %fusion.5.refs_0_.slot_ref, bf16[144,1536]{1,0:T(8,128)(2,1)} %collective-permute-done.6.refs_1_, bf16[144,1536]{1,0:T(8,128)(2,1)} %copy-done.29, bf16[144,1536]{1,0:T(8,128)(2,1)} %collective-permute-done.8.refs_3_, ...), custom_call_target="tpu_custom_call" | custom-call | flops 13000 | tf_op jit(solution)/shard_map/cotangent/pallas_call | solution.py:655
  127.9 6.1 %collective-permute-done.15.refs_1_ = bf16[128,1536]{1,0:T(8,128)(2,1)S(1)} collective-permute-done((bf16[128,1536]{1,0:T(8,128)(2,1)S(1)}, bf16[128,1536]{1,0:T(8,128)(2,1)S(1)}, u32[]{:S(2)}, u32[]{:S(2)}) %collective-permute-start.15) | collective-permute-done | bytes 393248 | tf_op jit(solution)/shard_map/ppermute | solution.py:22
  134.9 21.2 %experts.2 = (bf16[10,160,1536]{2,1,0:T(8,128)(2,1)}, bf16[10,160,256]{2,1,0:T(8,128)(2,1)}, bf16[10,160,256]{2,1,0:T(8,128)(2,1)}, bf16[10,160,256]{2,1,0:T(8,1...) custom-call(s32[1]{0:T(128)} %bitcast.2.place_ref, s32[2,10,256]{2,1,0:T(8,128)} %get-tuple-element.273.slot_ref, ...), custom_call_target="tpu_custom_call" | custom-call | flops 18000 | tf_op jit(solution)/shard_map/experts/pallas_call | solution.py:683
  156.7 21.3 %experts.3 = (bf16[10,160,1536]{2,1,0:T(8,128)(2,1)}, bf16[10,160,256]{2,1,0:T(8,128)(2,1)}, bf16[10,160,256]{2,1,0:T(8,128)(2,1)}, bf16[10,160,256]{2,1,0:T(8,1...) custom-call(s32[1]{0:T(128)} %bitcast.2.place_ref, s32[2,10,256]{2,1,0:T(8,128)} %get-tuple-element.272.slot_ref, ...), custom_call_target="tpu_custom_call" | custom-call | flops 18000 | tf_op jit(solution)/shard_map/experts/pallas_call | solution.py:683
  184.3 14.7 %combine.1 = (bf16[4,256,768]{2,1,0:T(8,128)(2,1)}, bf16[4,256,768]{2,1,0:T(8,128)(2,1)}) custom-call(s32[2]{0:T(128)} %pad_add_fusion.1.where_ref, s32[4,10,256]{2,1,0:T(8,128)} %fusion.5.refs_0_.slot_ref, bf16[10,160,256]{2,1,0:T(8,128)(2,1)} %get-tuple-element.129.ga_ref.refs_1_, bf16[10,160,256]{2,1,0:T(8,128)(2,1)} %get-tuple-element.130.gb_ref.refs_5_, ...), custom_call_target="tpu_custom_call" | custom-call | flops 12000 | tf_op jit(solution)/shard_map/combine/pallas_call | solution.py:747
  199.0 6.0 %weights.3 = bf16[4,2,3,384,256]{4,3,2,1,0:T(8,128)(2,1)} custom-call(s32[1]{0:T(128)} %bitcast.12.own_ref.where_ref, bf16[10,320,1536]{2,1,0:T(8,128)(2,1)} %get-tuple-element.135.cg_ref, bf16[10,160,1536]{2,1,0:T(8,128)(2,1)} %get-tuple-element.136.refs_0_, bf16[10,160,256]{2,1,0:T(8,128)(2,1)} %get-tuple-element.129.ga_ref.refs_1_, ...), custom_call_target="tpu_custom_call" | custom-call | flops 12000 | tf_op jit(solution)/shard_map/weights/pallas_call | solution.py:778
  207.3 18.1 %weights.4 = bf16[4,7,3,384,256]{4,3,2,1,0:T(8,128)(2,1)} custom-call(s32[1]{0:T(128)} %bitcast.12.own_ref.where_ref, bf16[10,320,1536]{2,1,0:T(8,128)(2,1)} %get-tuple-element.135.cg_ref, bf16[10,160,1536]{2,1,0:T(8,128)(2,1)} %get-tuple-element.136.refs_0_, bf16[10,160,256]{2,1,0:T(8,128)(2,1)} %get-tuple-element.129.ga_ref.refs_1_, ...), custom_call_target="tpu_custom_call" | custom-call | flops 12000 | tf_op jit(solution)/shard_map/weights/pallas_call | solution.py:778
  229.7 8.9 %collective-permute-done.22 = bf16[4,256,768]{2,1,0:T(8,128)(2,1)} collective-permute-done((bf16[4,256,768]{2,1,0:T(8,128)(2,1)}, bf16[4,256,768]{2,1,0:T(8,128)(2,1)}, u32[]{:S(2)}, u32[]{:S(2)}) %collective-permute-start.22) | collective-permute-done | bytes 1572896 | tf_op jit(solution)/shard_map/ppermute | solution.py:22
  247.5 7.8 %collective-permute-done.24.far_ref = bf16[144,1536]{1,0:T(8,128)(2,1)S(1)} collective-permute-done((bf16[144,1536]{1,0:T(8,128)(2,1)S(1)}, bf16[144,1536]{1,0:T(8,128)(2,1)S(1)}, u32[]{:S(2)}, u32[]{:S(2)}) %collective-permute-start.24) | collective-permute-done | bytes 442400 | tf_op jit(solution)/shard_map/ppermute | solution.py:22
  256.1 8.3 %norm_grad.1 = (f32[256,1536]{1,0:T(8,128)}, bf16[256,1536]{1,0:T(8,128)(2,1)}, bf16[256,1536]{1,0:T(8,128)(2,1)}, bf16[256,768]{1,0:T(8,128)(2,1)}, bf16[256,128]{1,0:T(8,128)(2,1)}) custom-call(s32[2]{0:T(128)} %pad_add_fusion.1.where_ref, bf16[144,1536]{1,0:T(8,128)(2,1)} %copy-done.8, bf16[144,1536]{1,0:T(8,128)(2,1)} %copy-done.32, ...), custom_call_target="tpu_custom_call" | custom-call | flops 4000 | tf_op jit(solution)/shard_map/norm_grad/pallas_call | solution.py:828
  264.4 11.9 %attend_grad.1 = (f32[256,768]{1,0:T(8,128)}, bf16[4,512,256]{2,1,0:T(8,128)(2,1)}) custom-call(s32[1]{0:T(128)} %bitcast.2.place_ref, bf16[256,768]{1,0:T(8,128)(2,1)} %get-tuple-element.109.refs_0_, bf16[256,512]{1,0:T(8,128)(2,1)} %get-tuple-element.110.refs_1_, bf16[256,512]{1,0:T(8,128)(2,1)} %copy-done.25, bf16[256,512]{1,0:T(8,128)(2,1)} %copy-done.24, ...), custom_call_target="tpu_custom_call" | custom-call | flops 10000 | tf_op jit(solution)/shard_map/attend_grad/pallas_call | solution.py:856
  276.2 7.7 %early.1 = (bf16[4,2,96,1664]{3,2,1,0:T(8,128)(2,1)}, bf16[4,2,96,1664]{3,2,1,0:T(8,128)(2,1)}, bf16[256,768]{1,0:T(8,128)(2,1)}) custom-call(s32[1]{0:T(128)} %bitcast.12.own_ref.where_ref, bf16[256,1536]{1,0:T(8,128)(2,1)} %get-tuple-element.159.low_ref, bf16[256,768]{1,0:T(8,128)(2,1)} %get-tuple-element.111.mine_ref.o_ref, bf16[256,1536]{1,0:T(8,128)(2,1)} %copy-done.6, ...), custom_call_target="tpu_custom_call" | custom-call | flops 5000 | tf_op jit(solution)/shard_map/early/pallas_call | solution.py:877
  284.7 5.0 %all-to-all-start.1 = ((bf16[4,512,256]{2,1,0:T(8,128)(2,1)}), bf16[4,512,256]{2,1,0:T(8,128)(2,1)S(1)}, u32[]{:S(2)}, u32[]{:S(2)}) async-start(bf16[4,512,256]{2,1,0:T(8,128)(2,1)} %get-tuple-element.169), calls=%async_computation.1 | async-start | bytes 2097152 | tf_op jit(solution)/shard_map/all_to_all | solution.py:53
  296.1 19.6 %all-to-all-done.1.kv_ref = bf16[4,512,256]{2,1,0:T(8,128)(2,1)S(1)} async-done(((bf16[4,512,256]{2,1,0:T(8,128)(2,1)}), bf16[4,512,256]{2,1,0:T(8,128)(2,1)S(1)}, u32[]{:S(2)}, u32[]{:S(2)}) %all-to-all-start.1) | async-done | bytes 1048608 | tf_op jit(solution)/shard_map/all_to_all | solution.py:53
  321.2 5.3 %input.1 = (bf16[256,512]{1,0:T(8,128)(2,1)}, bf16[256,1536]{1,0:T(8,128)(2,1)}, f32[16,1536]{1,0:T(8,128)}) custom-call(bf16[256,768]{1,0:T(8,128)(2,1)} %get-tuple-element.167.dq_ref, bf16[4,512,256]{2,1,0:T(8,128)(2,1)} %copy-done.17, f32[256,128]{1,0:T(8,128)} %get-tuple-element.277.cos_ref, f32[256,128]{1,0:T(8,128)} %get-tuple-element.276.sin_ref, ...), custom_call_target="tpu_custom_call" | custom-call | flops 4000 | tf_op jit(solution)/shard_map/input/pallas_call | solution.py:900
  328.5 18.8 %collective-permute-done.27.other_ref = f32[16,1536]{1,0:T(8,128)S(1)} collective-permute-done((f32[16,1536]{1,0:T(8,128)}, f32[16,1536]{1,0:T(8,128)S(1)}, u32[]{:S(2)}, u32[]{:S(2)}) %collective-permute-start.27) | collective-permute-done | bytes 98336 | tf_op jit(solution)/shard_map/ppermute | solution.py:22
  357.9 21.0 %all-to-all-done.2 = bf16[4,2,96,1664]{3,2,1,0:T(8,128)(2,1)} async-done(((bf16[4,2,96,1664]{3,2,1,0:T(8,128)(2,1)}), bf16[4,2,96,1664]{3,2,1,0:T(8,128)(2,1)}, u32[]{:S(2)}, u32[]{:S(2)}) %all-to-all-start.2) | async-done | bytes 2555936 | tf_op jit(solution)/shard_map/all_to_all | solution.py:53
  411.7 7.2 %collective-permute-done.30.refs_2_ = bf16[1,3,384,256]{3,2,1,0:T(8,128)(2,1)} collective-permute-done((bf16[1,3,384,256]{3,2,1,0:T(8,128)(2,1)}, bf16[1,3,384,256]{3,2,1,0:T(8,128)(2,1)}, u32[]{:S(2)}, u32[]{:S(2)}) %collective-permute-start.30) | collective-permute-done | bytes 589856 | tf_op jit(solution)/shard_map/ppermute | solution.py:22
  (218 shorter events, 143.1 us)
Async XLA Ops:
  7.2 388.3 %reduce-scatter.5.cloned.1.call-start = ((), (), s32[]{:S(2)}) async-start(), calls=%async_computation.7 | async-start | bytes 5898240 | tf_op jit(solution)/shard_map/reduce_scatter | solution.py:804
  8.6 29.1 %collective-permute-start = (bf16[384,1536]{1,0:T(8,128)(2,1)S(1)}, bf16[384,1536]{1,0:T(8,128)(2,1)}, u32[]{:S(2)}, u32[]{:S(2)}) collective-permute-start(bf16[384,1536]{1,0:T(8,128)(2,1)S(1)} %constant_dynamic-slice_fusion.2), channel_id=1, source_target_pairs={{0,1},{1,0},{2,3},{3,2},{4,5},{5,4},{6,7},{7,6},{8,9},{9,8},{10,11... | collective-permute-start | bytes 3538952 | tf_op jit(solution)/shard_map/ppermute | solution.py:22
  37.7 33.5 %collective-permute-start.5 = (bf16[384,1536]{1,0:T(8,128)(2,1)}, bf16[384,1536]{1,0:T(8,128)(2,1)}, u32[]{:S(2)}, u32[]{:S(2)}) collective-permute-start(bf16[384,1536]{1,0:T(8,128)(2,1)} %collective-permute-done.w_near), channel_id=1, source_target_pairs={{0,8},{8,0},{16,24},{24,16},{1,9},{9,1},{17,25},{25,17},{2,10},{10... | collective-permute-start | bytes 3538952 | tf_op jit(solution)/shard_map/ppermute | solution.py:22
  40.0 40.2 %collective-permute-start.8 = (bf16[144,1536]{1,0:T(8,128)(2,1)}, bf16[144,1536]{1,0:T(8,128)(2,1)}, u32[]{:S(2)}, u32[]{:S(2)}) collective-permute-start(bf16[144,1536]{1,0:T(8,128)(2,1)} %fusion.13.refs_7_), channel_id=1, source_target_pairs={{0,2},{2,4},{4,6},{6,0},{1,3},{3,5},{5,7},{7,1},{8,10},{10,12},{12... | collective-permute-start | bytes 1327112 | tf_op jit(solution)/shard_map/ppermute | solution.py:27
  46.1 33.6 %collective-permute-start.6 = (bf16[144,1536]{1,0:T(8,128)(2,1)}, bf16[144,1536]{1,0:T(8,128)(2,1)}, u32[]{:S(2)}, u32[]{:S(2)}) collective-permute-start(bf16[144,1536]{1,0:T(8,128)(2,1)} %fusion.13.refs_7_), channel_id=1, source_target_pairs={{0,6},{2,0},{4,2},{6,4},{1,7},{3,1},{5,3},{7,5},{8,14},{10,8},{12,... | collective-permute-start | bytes 1327112 | tf_op jit(solution)/shard_map/ppermute | solution.py:27
  61.9 29.3 %collective-permute-start.10 = (bf16[144,1536]{1,0:T(8,128)(2,1)}, bf16[144,1536]{1,0:T(8,128)(2,1)}, u32[]{:S(2)}, u32[]{:S(2)}) collective-permute-start(bf16[144,1536]{1,0:T(8,128)(2,1)} %fusion.13.refs_7_), channel_id=1, source_target_pairs={{0,4},{2,6},{4,0},{6,2},{1,5},{3,7},{5,1},{7,3},{8,12},{10,14},{12... | collective-permute-start | bytes 1327112 | tf_op jit(solution)/shard_map/ppermute | solution.py:27
  79.7 25.5 %collective-permute-start.7 = (bf16[144,1536]{1,0:T(8,128)(2,1)}, bf16[144,1536]{1,0:T(8,128)(2,1)S(1)}, u32[]{:S(2)}, u32[]{:S(2)}) collective-permute-start(bf16[144,1536]{1,0:T(8,128)(2,1)} %collective-permute-done.6.refs_1_), channel_id=1, source_target_pairs={{0,1},{1,0},{2,3},{3,2},{4,5},{5,4},{6,7},{7,6},{8,9},{9,8},{10,11... | collective-permute-start | bytes 1327112 | tf_op jit(solution)/shard_map/ppermute | solution.py:22
  80.3 26.5 %collective-permute-start.9 = (bf16[144,1536]{1,0:T(8,128)(2,1)}, bf16[144,1536]{1,0:T(8,128)(2,1)S(1)}, u32[]{:S(2)}, u32[]{:S(2)}) collective-permute-start(bf16[144,1536]{1,0:T(8,128)(2,1)} %collective-permute-done.8.refs_3_), channel_id=1, source_target_pairs={{0,1},{1,0},{2,3},{3,2},{4,5},{5,4},{6,7},{7,6},{8,9},{9,8},{10,11... | collective-permute-start | bytes 1327112 | tf_op jit(solution)/shard_map/ppermute | solution.py:22
  101.7 24.4 %collective-permute-start.14 = (bf16[128,1536]{1,0:T(8,128)(2,1)S(1)}, bf16[128,1536]{1,0:T(8,128)(2,1)S(1)}, u32[]{:S(2)}, u32[]{:S(2)}) collective-permute-start(bf16[128,1536]{1,0:T(8,128)(2,1)S(1)} %get-tuple-element.118.refs_2_), channel_id=1, source_target_pairs={{0,4},{2,6},{4,0},{6,2},{1,5},{3,7},{5,1},{7,3},{8,12},{10,14},{12... | collective-permute-start | bytes 1179656 | tf_op jit(solution)/shard_map/ppermute | solution.py:27
  104.7 29.3 %collective-permute-start.17 = (bf16[128,1536]{1,0:T(8,128)(2,1)S(1)}, bf16[128,1536]{1,0:T(8,128)(2,1)S(1)}, u32[]{:S(2)}, u32[]{:S(2)}) collective-permute-start(bf16[128,1536]{1,0:T(8,128)(2,1)S(1)} %collective-permute-done.13.refs_2_), channel_id=1, source_target_pairs={{0,1},{1,0},{2,3},{3,2},{4,5},{5,4},{6,7},{7,6},{8,9},{9,8},{10,11... | collective-permute-start | bytes 1179656 | tf_op jit(solution)/shard_map/ppermute | solution.py:22
  105.2 28.8 %collective-permute-start.16 = (bf16[128,1536]{1,0:T(8,128)(2,1)S(1)}, bf16[128,1536]{1,0:T(8,128)(2,1)S(1)}, u32[]{:S(2)}, u32[]{:S(2)}) collective-permute-start(bf16[128,1536]{1,0:T(8,128)(2,1)S(1)} %collective-permute-done.12.refs_0_), channel_id=1, source_target_pairs={{0,1},{1,0},{2,3},{3,2},{4,5},{5,4},{6,7},{7,6},{8,9},{9,8},{10,11... | collective-permute-start | bytes 1179656 | tf_op jit(solution)/shard_map/ppermute | solution.py:22
  156.2 23.5 %collective-permute-start.18 = (bf16[2,144,1536]{2,1,0:T(8,128)(2,1)}, bf16[2,144,1536]{2,1,0:T(8,128)(2,1)S(1)}, u32[]{:S(2)}, u32[]{:S(2)}) collective-permute-start(bf16[2,144,1536]{2,1,0:T(8,128)(2,1)} %get-tuple-element.123), channel_id=1, source_target_pairs={{0,1},{1,0},{2,3},{3,2},{4,5},{5,4},{6,7},{7,6},{8,9},{9,8},{10,11... | collective-permute-start | bytes 2654216 | tf_op jit(solution)/shard_map/ppermute | solution.py:22
  178.0 27.1 %collective-permute-start.19 = (bf16[2,144,1536]{2,1,0:T(8,128)(2,1)}, bf16[2,144,1536]{2,1,0:T(8,128)(2,1)S(1)}, u32[]{:S(2)}, u32[]{:S(2)}) collective-permute-start(bf16[2,144,1536]{2,1,0:T(8,128)(2,1)} %get-tuple-element.133), channel_id=1, source_target_pairs={{0,1},{1,0},{2,3},{3,2},{4,5},{5,4},{6,7},{7,6},{8,9},{9,8},{10,11... | collective-permute-start | bytes 2654216 | tf_op jit(solution)/shard_map/ppermute | solution.py:22
  179.9 25.2 %collective-permute-start.20 = (bf16[144,1536]{1,0:T(8,128)(2,1)S(1)}, bf16[144,1536]{1,0:T(8,128)(2,1)S(1)}, u32[]{:S(2)}, u32[]{:S(2)}) collective-permute-start(bf16[144,1536]{1,0:T(8,128)(2,1)S(1)} %get-tuple-element.124), channel_id=1, source_target_pairs={{0,2},{2,4},{4,6},{6,0},{1,3},{3,5},{5,7},{7,1},{8,10},{10,12},{12... | collective-permute-start | bytes 1327112 | tf_op jit(solution)/shard_map/ppermute | solution.py:32
  183.3 21.8 %collective-permute-start.21 = (bf16[144,1536]{1,0:T(8,128)(2,1)S(1)}, bf16[144,1536]{1,0:T(8,128)(2,1)S(1)}, u32[]{:S(2)}, u32[]{:S(2)}) collective-permute-start(bf16[144,1536]{1,0:T(8,128)(2,1)S(1)} %get-tuple-element.125), channel_id=1, source_target_pairs={{0,6},{2,0},{4,2},{6,4},{1,7},{3,1},{5,3},{7,5},{8,14},{10,8},{12,... | collective-permute-start | bytes 1327112 | tf_op jit(solution)/shard_map/ppermute | solution.py:32
  205.4 199.8 %reduce-scatter.3.cloned.1.call-start = ((), (), s32[]{:S(2)}) async-start(), calls=%async_computation.6 | async-start | bytes 20643840 | tf_op jit(solution)/shard_map/reduce_scatter | solution.py:816
  205.4 33.2 %collective-permute-start.22 = (bf16[4,256,768]{2,1,0:T(8,128)(2,1)}, bf16[4,256,768]{2,1,0:T(8,128)(2,1)}, u32[]{:S(2)}, u32[]{:S(2)}) collective-permute-start(bf16[4,256,768]{2,1,0:T(8,128)(2,1)} %get-tuple-element.144), channel_id=1, source_target_pairs={{0,1},{1,0},{2,3},{3,2},{4,5},{5,4},{6,7},{7,6},{8,9},{9,8},{10,11... | collective-permute-start | bytes 4718600 | tf_op jit(solution)/shard_map/ppermute | solution.py:22
  205.9 36.1 %collective-permute-start.23 = (bf16[144,1536]{1,0:T(8,128)(2,1)S(1)}, bf16[144,1536]{1,0:T(8,128)(2,1)S(1)}, u32[]{:S(2)}, u32[]{:S(2)}) collective-permute-start(bf16[144,1536]{1,0:T(8,128)(2,1)S(1)} %get-tuple-element.143), channel_id=1, source_target_pairs={{0,4},{2,6},{4,0},{6,2},{1,5},{3,7},{5,1},{7,3},{8,12},{10,14},{12... | collective-permute-start | bytes 1327112 | tf_op jit(solution)/shard_map/ppermute | solution.py:32
  242.4 42.4 %all-to-all-start = ((bf16[4,256,768]{2,1,0:T(8,128)(2,1)}), bf16[4,256,768]{2,1,0:T(8,128)(2,1)}, u32[]{:S(2)}, u32[]{:S(2)}) async-start(bf16[4,256,768]{2,1,0:T(8,128)(2,1)} %add_convert_fusion.1), calls=%async_computation | async-start | bytes 3145728 | tf_op jit(solution)/shard_map/all_to_all | solution.py:53
  284.7 30.9 %all-to-all-start.1 = ((bf16[4,512,256]{2,1,0:T(8,128)(2,1)}), bf16[4,512,256]{2,1,0:T(8,128)(2,1)S(1)}, u32[]{:S(2)}, u32[]{:S(2)}) async-start(bf16[4,512,256]{2,1,0:T(8,128)(2,1)} %get-tuple-element.169), calls=%async_computation.1 | async-start | bytes 2097152 | tf_op jit(solution)/shard_map/all_to_all | solution.py:53
  316.6 62.2 %all-to-all-start.2 = ((bf16[4,2,96,1664]{3,2,1,0:T(8,128)(2,1)}), bf16[4,2,96,1664]{3,2,1,0:T(8,128)(2,1)}, u32[]{:S(2)}, u32[]{:S(2)}) async-start(bf16[4,2,96,1664]{3,2,1,0:T(8,128)(2,1)} %add_convert_fusion), calls=%async_computation.2 | async-start | bytes 5111808 | tf_op jit(solution)/shard_map/all_to_all | solution.py:53
  326.5 25.6 %collective-permute-start.28 = (bf16[256,1536]{1,0:T(8,128)(2,1)}, bf16[256,1536]{1,0:T(8,128)(2,1)S(1)}, u32[]{:S(2)}, u32[]{:S(2)}) collective-permute-start(bf16[256,1536]{1,0:T(8,128)(2,1)} %get-tuple-element.176), channel_id=1, source_target_pairs={{0,1},{1,0},{2,3},{3,2},{4,5},{5,4},{6,7},{7,6},{8,9},{9,8},{10,11... | collective-permute-start | bytes 2359304 | tf_op jit(solution)/shard_map/ppermute | solution.py:22
  382.1 39.1 %all-to-all-start.3 = ((bf16[8,96,640]{2,1,0:T(8,128)(2,1)}), bf16[8,96,640]{2,1,0:T(8,128)(2,1)}, u32[]{:S(2)}, u32[]{:S(2)}) async-start(bf16[8,96,640]{2,1,0:T(8,128)(2,1)} %add_convert_fusion.2), calls=%async_computation.3 | async-start | bytes 1966080 | tf_op jit(solution)/shard_map/all_to_all | solution.py:922
  392.2 26.7 %collective-permute-start.30 = (bf16[1,3,384,256]{3,2,1,0:T(8,128)(2,1)}, bf16[1,3,384,256]{3,2,1,0:T(8,128)(2,1)}, u32[]{:S(2)}, u32[]{:S(2)}) collective-permute-start(bf16[1,3,384,256]{3,2,1,0:T(8,128)(2,1)} %fusion.12), channel_id=1, source_target_pairs={{0,16},{8,24},{16,0},{24,8},{1,17},{9,25},{17,1},{25,9},{2,18},{10... | collective-permute-start | bytes 1769480 | tf_op jit(solution)/shard_map/ppermute | solution.py:22
  (58 other events, 652.6 us)
Sparse Core Ops, SparseCore 0:
  205.5 46.0 reduce-scatter.4
  254.4 124.5 reduce-scatter.2
where the time goes:
time: 436 us; the launch traced here: 431 us
  Pallas kernels  166 us (38%)
  waiting for transfers between devices  131 us (30%)
  starting transfers between devices  61.7 us (14%)
  other arithmetic  29.6 us (7%)
  local copies, waits for them, and re-layouts  27.1 us (6%)
  between operations  14.8 us (3%)
    ppermute x20, waiting for transfers between devices, swap(): return lax.ppermute(values, axis, [(i, i ^ bit) for i in range(count)])  79 us
    pallas_call x2, Pallas kernels, run_experts(): pl.pallas_call(functools.partial(experts_kernel, group, capacity), name='...  42.5 us
    all_to_all x3, waiting for transfers between devices, exchange(): lax.all_to_all(parts, 'expert', split_axis=0, concat_axis=0, tiled=True)  40.5 us
    pallas_call x3, Pallas kernels, weights(): pl.pallas_call(weights_kernel, name='weights', grid_spec=prefetch(num_sca...  28.5 us
    ppermute x9, starting transfers between devices, fetch(): lax.ppermute(values, 'expert', [(i, (i - offset) % count) for i in range(...  20.8 us
    ppermute x20, starting transfers between devices, swap(): return lax.ppermute(values, axis, [(i, i ^ bit) for i in range(count)])  17.2 us
    pallas_call x1, Pallas kernels, body(): pl.pallas_call(functools.partial(cotangent_kernel, n_exp, capacity), name...  14.7 us
    pallas_call x1, Pallas kernels, combine(): pl.pallas_call(functools.partial(combine_kernel, capacity, order), name='...  14.7 us
  transfers between devices with their start and end apart: 38, of which 15 were waited for; matrix products, arithmetic and copies ran while one was open for 10% of the time, Pallas kernels for 34%

commit v1 on v0

--- a/solution.py
+++ b/solution.py
@@ -940,7 +940,7 @@
                 shaped(F32, experts_local, inner, slice_width),
             ),
             input_output_aliases={len(totals) + i: i for i in range(len(earlier))},
-            compiler_params=params(24),
+            compiler_params=params(),
             cost_estimate=cost(3),
         )(*totals, *earlier)
 

time: 436 us -> 431 us (0.989)
  Pallas kernels: 166 us -> 171 us
  transfers between devices with their start and end apart: 38 -> 38, of which waited for: 15 -> 15; matrix products, arithmetic and copies ran while one was open for 10% -> 9% of each run, Pallas kernels for 34% -> 35%
where the time goes in v1:
time: 431 us; the launch traced here: 426 us
  Pallas kernels  171 us (40%)
  waiting for transfers between devices  132 us (31%)
  starting transfers between devices  59.4 us (14%)
  other arithmetic  25.4 us (6%)
  local copies, waits for them, and re-layouts  23.7 us (5%)
  between operations  14.8 us (3%)
    ppermute x20, waiting for transfers between devices, swap(): return lax.ppermute(values, axis, [(i, i ^ bit) for i in range(count)])  81.6 us
    pallas_call x2, Pallas kernels, run_experts(): pl.pallas_call(functools.partial(experts_kernel, group, capacity), name='...  42.5 us
    all_to_all x3, waiting for transfers between devices, exchange(): lax.all_to_all(parts, 'expert', split_axis=0, concat_axis=0, tiled=True)  38.5 us
    pallas_call x3, Pallas kernels, weights(): pl.pallas_call(weights_kernel, name='weights', grid_spec=prefetch(num_sca...  28.4 us
    ppermute x9, starting transfers between devices, fetch(): lax.ppermute(values, 'expert', [(i, (i - offset) % count) for i in range(...  20.8 us
    ppermute x20, starting transfers between devices, swap(): return lax.ppermute(values, axis, [(i, i ^ bit) for i in range(count)])  17.2 us
    pallas_call x1, Pallas kernels, body(): pl.pallas_call(functools.partial(cotangent_kernel, n_exp, capacity), name...  14.7 us
    pallas_call x1, Pallas kernels, combine(): pl.pallas_call(functools.partial(combine_kernel, capacity, order), name='...  14.7 us
  transfers between devices with their start and end apart: 38, of which 15 were waited for; matrix products, arithmetic and copies ran while one was open for 9% of the time, Pallas kernels for 35%

profile of v1, /device:TPU:0, one launch (start us, length us, event | category | flops | bytes accessed | tf_op | source)
XLA Modules:
  0.0 426.3 jit_solution(11670285773895013329)
XLA Ops:
  24.4 13.3 %collective-permute-done.w_near = bf16[384,1536]{1,0:T(8,128)(2,1)} collective-permute-done((bf16[384,1536]{1,0:T(8,128)(2,1)S(1)}, bf16[384,1536]{1,0:T(8,128)(2,1)}, u32[]{:S(2)}, u32[]{:S(2)}) %collective-permute-start) | collective-permute-done | bytes 1179680 | tf_op jit(solution)/shard_map/ppermute | solution.py:22
  40.0 6.1 %collective-permute-start.8 = (bf16[144,1536]{1,0:T(8,128)(2,1)}, bf16[144,1536]{1,0:T(8,128)(2,1)}, u32[]{:S(2)}, u32[]{:S(2)}) collective-permute-start(bf16[144,1536]{1,0:T(8,128)(2,1)} %fusion.13.refs_7_), channel_id=1, source_target_pairs={{0,2},{2,4},{4,6},{6,0},{1,3},{3,5},{5,7},{7,1},{8,10},{10,12},{12... | collective-permute-start | bytes 1327112 | tf_op jit(solution)/shard_map/ppermute | solution.py:27
  50.6 10.8 %attend.1 = (f32[256,768]{1,0:T(8,128)}, bf16[256,768]{1,0:T(8,128)(2,1)}, f32[256,12]{1,0:T(8,128)}) custom-call(bf16[256,768]{1,0:T(8,128)(2,1)} %get-tuple-element.109.refs_0_, bf16[256,512]{1,0:T(8,128)(2,1)} %get-tuple-element.110.refs_1_, bf16[256,512]{1,0:T(8,128)(2,1)} %copy-done.25, bf16[256,512]{1,0:T(8,128)(2,1)} %copy-done.24, ...), custom_call_target="tpu_custom_call" | custom-call | flops 10000 | tf_op jit(solution)/shard_map/attend/pallas_call | solution.py:578
  62.5 8.7 %collective-permute-done.4.other_ref = bf16[256,768]{1,0:T(8,128)(2,1)S(1)} collective-permute-done((bf16[256,768]{1,0:T(8,128)(2,1)}, bf16[256,768]{1,0:T(8,128)(2,1)S(1)}, u32[]{:S(2)}, u32[]{:S(2)}) %collective-permute-start.4) | collective-permute-done | bytes 393248 | tf_op jit(solution)/shard_map/ppermute | solution.py:22
  96.2 5.5 %collective-permute-done.12.refs_0_ = bf16[128,1536]{1,0:T(8,128)(2,1)S(1)} collective-permute-done((bf16[128,1536]{1,0:T(8,128)(2,1)S(1)}, bf16[128,1536]{1,0:T(8,128)(2,1)S(1)}, u32[]{:S(2)}, u32[]{:S(2)}) %collective-permute-start.12) | collective-permute-done | bytes 393248 | tf_op jit(solution)/shard_map/ppermute | solution.py:27
  111.4 14.7 %cotangent.1 = (bf16[10,320,1536]{2,1,0:T(8,128)(2,1)}, f32[10,320,256]{2,1,0:T(8,128)}) custom-call(s32[4,10,256]{2,1,0:T(8,128)} %fusion.5.refs_0_.slot_ref, bf16[144,1536]{1,0:T(8,128)(2,1)} %collective-permute-done.6.refs_1_, bf16[144,1536]{1,0:T(8,128)(2,1)} %copy-done.29, bf16[144,1536]{1,0:T(8,128)(2,1)} %collective-permute-done.8.refs_3_, ...), custom_call_target="tpu_custom_call" | custom-call | flops 13000 | tf_op jit(solution)/shard_map/cotangent/pallas_call | solution.py:655
  127.9 6.1 %collective-permute-done.15.refs_1_ = bf16[128,1536]{1,0:T(8,128)(2,1)S(1)} collective-permute-done((bf16[128,1536]{1,0:T(8,128)(2,1)S(1)}, bf16[128,1536]{1,0:T(8,128)(2,1)S(1)}, u32[]{:S(2)}, u32[]{:S(2)}) %collective-permute-start.15) | collective-permute-done | bytes 393248 | tf_op jit(solution)/shard_map/ppermute | solution.py:22
  134.9 21.2 %experts.2 = (bf16[10,160,1536]{2,1,0:T(8,128)(2,1)}, bf16[10,160,256]{2,1,0:T(8,128)(2,1)}, bf16[10,160,256]{2,1,0:T(8,128)(2,1)}, bf16[10,160,256]{2,1,0:T(8,1...) custom-call(s32[1]{0:T(128)} %bitcast.2.place_ref, s32[2,10,256]{2,1,0:T(8,128)} %get-tuple-element.273.slot_ref, ...), custom_call_target="tpu_custom_call" | custom-call | flops 18000 | tf_op jit(solution)/shard_map/experts/pallas_call | solution.py:683
  156.7 21.3 %experts.3 = (bf16[10,160,1536]{2,1,0:T(8,128)(2,1)}, bf16[10,160,256]{2,1,0:T(8,128)(2,1)}, bf16[10,160,256]{2,1,0:T(8,128)(2,1)}, bf16[10,160,256]{2,1,0:T(8,1...) custom-call(s32[1]{0:T(128)} %bitcast.2.place_ref, s32[2,10,256]{2,1,0:T(8,128)} %get-tuple-element.272.slot_ref, ...), custom_call_target="tpu_custom_call" | custom-call | flops 18000 | tf_op jit(solution)/shard_map/experts/pallas_call | solution.py:683
  184.3 14.7 %combine.1 = (bf16[4,256,768]{2,1,0:T(8,128)(2,1)}, bf16[4,256,768]{2,1,0:T(8,128)(2,1)}) custom-call(s32[2]{0:T(128)} %pad_add_fusion.1.where_ref, s32[4,10,256]{2,1,0:T(8,128)} %fusion.5.refs_0_.slot_ref, bf16[10,160,256]{2,1,0:T(8,128)(2,1)} %get-tuple-element.129.ga_ref.refs_1_, bf16[10,160,256]{2,1,0:T(8,128)(2,1)} %get-tuple-element.130.gb_ref.refs_5_, ...), custom_call_target="tpu_custom_call" | custom-call | flops 12000 | tf_op jit(solution)/shard_map/combine/pallas_call | solution.py:747
  199.0 6.0 %weights.3 = bf16[4,2,3,384,256]{4,3,2,1,0:T(8,128)(2,1)} custom-call(s32[1]{0:T(128)} %bitcast.12.own_ref.where_ref, bf16[10,320,1536]{2,1,0:T(8,128)(2,1)} %get-tuple-element.135.cg_ref, bf16[10,160,1536]{2,1,0:T(8,128)(2,1)} %get-tuple-element.136.refs_0_, bf16[10,160,256]{2,1,0:T(8,128)(2,1)} %get-tuple-element.129.ga_ref.refs_1_, ...), custom_call_target="tpu_custom_call" | custom-call | flops 12000 | tf_op jit(solution)/shard_map/weights/pallas_call | solution.py:778
  207.3 18.1 %weights.4 = bf16[4,7,3,384,256]{4,3,2,1,0:T(8,128)(2,1)} custom-call(s32[1]{0:T(128)} %bitcast.12.own_ref.where_ref, bf16[10,320,1536]{2,1,0:T(8,128)(2,1)} %get-tuple-element.135.cg_ref, bf16[10,160,1536]{2,1,0:T(8,128)(2,1)} %get-tuple-element.136.refs_0_, bf16[10,160,256]{2,1,0:T(8,128)(2,1)} %get-tuple-element.129.ga_ref.refs_1_, ...), custom_call_target="tpu_custom_call" | custom-call | flops 12000 | tf_op jit(solution)/shard_map/weights/pallas_call | solution.py:778
  229.6 9.0 %collective-permute-done.22 = bf16[4,256,768]{2,1,0:T(8,128)(2,1)} collective-permute-done((bf16[4,256,768]{2,1,0:T(8,128)(2,1)}, bf16[4,256,768]{2,1,0:T(8,128)(2,1)}, u32[]{:S(2)}, u32[]{:S(2)}) %collective-permute-start.22) | collective-permute-done | bytes 1572896 | tf_op jit(solution)/shard_map/ppermute | solution.py:22
  246.7 7.8 %collective-permute-done.24.far_ref = bf16[144,1536]{1,0:T(8,128)(2,1)S(1)} collective-permute-done((bf16[144,1536]{1,0:T(8,128)(2,1)S(1)}, bf16[144,1536]{1,0:T(8,128)(2,1)S(1)}, u32[]{:S(2)}, u32[]{:S(2)}) %collective-permute-start.24) | collective-permute-done | bytes 442400 | tf_op jit(solution)/shard_map/ppermute | solution.py:22
  255.3 8.3 %norm_grad.1 = (f32[256,1536]{1,0:T(8,128)}, bf16[256,1536]{1,0:T(8,128)(2,1)}, bf16[256,1536]{1,0:T(8,128)(2,1)}, bf16[256,768]{1,0:T(8,128)(2,1)}, bf16[256,128]{1,0:T(8,128)(2,1)}) custom-call(s32[2]{0:T(128)} %pad_add_fusion.1.where_ref, bf16[144,1536]{1,0:T(8,128)(2,1)} %copy-done.6, bf16[144,1536]{1,0:T(8,128)(2,1)} %copy-done.32, ...), custom_call_target="tpu_custom_call" | custom-call | flops 4000 | tf_op jit(solution)/shard_map/norm_grad/pallas_call | solution.py:828
  263.6 11.9 %attend_grad.1 = (f32[256,768]{1,0:T(8,128)}, bf16[4,512,256]{2,1,0:T(8,128)(2,1)}) custom-call(s32[1]{0:T(128)} %bitcast.2.place_ref, bf16[256,768]{1,0:T(8,128)(2,1)} %get-tuple-element.109.refs_0_, bf16[256,512]{1,0:T(8,128)(2,1)} %get-tuple-element.110.refs_1_, bf16[256,512]{1,0:T(8,128)(2,1)} %copy-done.25, bf16[256,512]{1,0:T(8,128)(2,1)} %copy-done.24, ...), custom_call_target="tpu_custom_call" | custom-call | flops 10000 | tf_op jit(solution)/shard_map/attend_grad/pallas_call | solution.py:856
  275.5 8.0 %early.1 = (bf16[4,2,96,1664]{3,2,1,0:T(8,128)(2,1)}, bf16[4,2,96,1664]{3,2,1,0:T(8,128)(2,1)}, bf16[256,768]{1,0:T(8,128)(2,1)}) custom-call(s32[1]{0:T(128)} %bitcast.12.own_ref.where_ref, bf16[256,1536]{1,0:T(8,128)(2,1)} %get-tuple-element.159.low_ref, bf16[256,768]{1,0:T(8,128)(2,1)} %get-tuple-element.111.mine_ref.o_ref, bf16[256,1536]{1,0:T(8,128)(2,1)} %copy-done.5, ...), custom_call_target="tpu_custom_call" | custom-call | flops 5000 | tf_op jit(solution)/shard_map/early/pallas_call | solution.py:877
  297.3 17.9 %all-to-all-done.1.kv_ref = bf16[4,512,256]{2,1,0:T(8,128)(2,1)S(1)} async-done(((bf16[4,512,256]{2,1,0:T(8,128)(2,1)}), bf16[4,512,256]{2,1,0:T(8,128)(2,1)S(1)}, u32[]{:S(2)}, u32[]{:S(2)}) %all-to-all-start.1) | async-done | bytes 1048608 | tf_op jit(solution)/shard_map/all_to_all | solution.py:53
  319.9 5.2 %input.1 = (bf16[256,512]{1,0:T(8,128)(2,1)}, bf16[256,1536]{1,0:T(8,128)(2,1)}, f32[16,1536]{1,0:T(8,128)}) custom-call(bf16[256,768]{1,0:T(8,128)(2,1)} %get-tuple-element.167.dq_ref, bf16[4,512,256]{2,1,0:T(8,128)(2,1)} %copy-done.15, f32[256,128]{1,0:T(8,128)} %get-tuple-element.277.cos_ref, f32[256,128]{1,0:T(8,128)} %get-tuple-element.276.sin_ref, ...), custom_call_target="tpu_custom_call" | custom-call | flops 4000 | tf_op jit(solution)/shard_map/input/pallas_call | solution.py:900
  327.1 18.8 %collective-permute-done.27.other_ref = f32[16,1536]{1,0:T(8,128)S(1)} collective-permute-done((f32[16,1536]{1,0:T(8,128)}, f32[16,1536]{1,0:T(8,128)S(1)}, u32[]{:S(2)}, u32[]{:S(2)}) %collective-permute-start.27) | collective-permute-done | bytes 98336 | tf_op jit(solution)/shard_map/ppermute | solution.py:22
  356.8 20.6 %all-to-all-done.2 = bf16[4,2,96,1664]{3,2,1,0:T(8,128)(2,1)S(1)} async-done(((bf16[4,2,96,1664]{3,2,1,0:T(8,128)(2,1)}), bf16[4,2,96,1664]{3,2,1,0:T(8,128)(2,1)S(1)}, u32[]{:S(2)}, u32[]{:S(2)}) %all-to-all-start.2) | async-done | bytes 2555936 | tf_op jit(solution)/shard_map/all_to_all | solution.py:53
  392.6 5.6 %collective-permute-done.31 = bf16[1,96,1664]{2,1,0:T(8,128)(2,1)S(1)} collective-permute-done((bf16[1,96,1664]{2,1,0:T(8,128)(2,1)}, bf16[1,96,1664]{2,1,0:T(8,128)(2,1)S(1)}, u32[]{:S(2)}, u32[]{:S(2)}) %collective-permute-start.31) | collective-permute-done | bytes 319520 | tf_op jit(solution)/shard_map/ppermute | solution.py:22
  400.5 7.2 %finish.4 = (f32[10,384,256]{2,1,0:T(8,128)}, f32[10,384,256]{2,1,0:T(8,128)}, f32[10,256,384]{2,1,0:T(8,128)}) custom-call(bf16[7,3,384,256]{3,2,1,0:T(8,128)(2,1)} %bitcast.41, f32[10,384,256]{2,1,0:T(8,128)} %get-tuple-element.192.refs_1_, f32[10,384,256]{2,1,0:T(8,128)} %get-tuple-element.193.refs_2_, ...), custom_call_target="tpu_custom_call", output_to_operand_aliasing={{0}: (1, {}), {1}: (2, {}), {2}: (3, {})} | custom-call | flops 3000 | tf_op jit(solution)/shard_map/finish/pallas_call | solution.py:931
  407.7 7.3 %collective-permute-done.30.refs_2_ = bf16[1,3,384,256]{3,2,1,0:T(8,128)(2,1)} collective-permute-done((bf16[1,3,384,256]{3,2,1,0:T(8,128)(2,1)}, bf16[1,3,384,256]{3,2,1,0:T(8,128)(2,1)}, u32[]{:S(2)}, u32[]{:S(2)}) %collective-permute-start.30) | collective-permute-done | bytes 589856 | tf_op jit(solution)/shard_map/ppermute | solution.py:22
  (218 shorter events, 137.3 us)
Async XLA Ops:
  7.2 382.8 %reduce-scatter.5.cloned.1.call-start = ((), (), s32[]{:S(2)}) async-start(), calls=%async_computation.7 | async-start | bytes 5898240 | tf_op jit(solution)/shard_map/reduce_scatter | solution.py:804
  8.6 29.1 %collective-permute-start = (bf16[384,1536]{1,0:T(8,128)(2,1)S(1)}, bf16[384,1536]{1,0:T(8,128)(2,1)}, u32[]{:S(2)}, u32[]{:S(2)}) collective-permute-start(bf16[384,1536]{1,0:T(8,128)(2,1)S(1)} %constant_dynamic-slice_fusion.2), channel_id=1, source_target_pairs={{0,1},{1,0},{2,3},{3,2},{4,5},{5,4},{6,7},{7,6},{8,9},{9,8},{10,11... | collective-permute-start | bytes 3538952 | tf_op jit(solution)/shard_map/ppermute | solution.py:22
  37.7 33.5 %collective-permute-start.5 = (bf16[384,1536]{1,0:T(8,128)(2,1)}, bf16[384,1536]{1,0:T(8,128)(2,1)}, u32[]{:S(2)}, u32[]{:S(2)}) collective-permute-start(bf16[384,1536]{1,0:T(8,128)(2,1)} %collective-permute-done.w_near), channel_id=1, source_target_pairs={{0,8},{8,0},{16,24},{24,16},{1,9},{9,1},{17,25},{25,17},{2,10},{10... | collective-permute-start | bytes 3538952 | tf_op jit(solution)/shard_map/ppermute | solution.py:22
  40.0 40.2 %collective-permute-start.8 = (bf16[144,1536]{1,0:T(8,128)(2,1)}, bf16[144,1536]{1,0:T(8,128)(2,1)}, u32[]{:S(2)}, u32[]{:S(2)}) collective-permute-start(bf16[144,1536]{1,0:T(8,128)(2,1)} %fusion.13.refs_7_), channel_id=1, source_target_pairs={{0,2},{2,4},{4,6},{6,0},{1,3},{3,5},{5,7},{7,1},{8,10},{10,12},{12... | collective-permute-start | bytes 1327112 | tf_op jit(solution)/shard_map/ppermute | solution.py:27
  46.1 33.6 %collective-permute-start.6 = (bf16[144,1536]{1,0:T(8,128)(2,1)}, bf16[144,1536]{1,0:T(8,128)(2,1)}, u32[]{:S(2)}, u32[]{:S(2)}) collective-permute-start(bf16[144,1536]{1,0:T(8,128)(2,1)} %fusion.13.refs_7_), channel_id=1, source_target_pairs={{0,6},{2,0},{4,2},{6,4},{1,7},{3,1},{5,3},{7,5},{8,14},{10,8},{12,... | collective-permute-start | bytes 1327112 | tf_op jit(solution)/shard_map/ppermute | solution.py:27
  61.9 29.3 %collective-permute-start.10 = (bf16[144,1536]{1,0:T(8,128)(2,1)}, bf16[144,1536]{1,0:T(8,128)(2,1)}, u32[]{:S(2)}, u32[]{:S(2)}) collective-permute-start(bf16[144,1536]{1,0:T(8,128)(2,1)} %fusion.13.refs_7_), channel_id=1, source_target_pairs={{0,4},{2,6},{4,0},{6,2},{1,5},{3,7},{5,1},{7,3},{8,12},{10,14},{12... | collective-permute-start | bytes 1327112 | tf_op jit(solution)/shard_map/ppermute | solution.py:27
  79.7 25.5 %collective-permute-start.7 = (bf16[144,1536]{1,0:T(8,128)(2,1)}, bf16[144,1536]{1,0:T(8,128)(2,1)S(1)}, u32[]{:S(2)}, u32[]{:S(2)}) collective-permute-start(bf16[144,1536]{1,0:T(8,128)(2,1)} %collective-permute-done.6.refs_1_), channel_id=1, source_target_pairs={{0,1},{1,0},{2,3},{3,2},{4,5},{5,4},{6,7},{7,6},{8,9},{9,8},{10,11... | collective-permute-start | bytes 1327112 | tf_op jit(solution)/shard_map/ppermute | solution.py:22
  80.3 26.5 %collective-permute-start.9 = (bf16[144,1536]{1,0:T(8,128)(2,1)}, bf16[144,1536]{1,0:T(8,128)(2,1)S(1)}, u32[]{:S(2)}, u32[]{:S(2)}) collective-permute-start(bf16[144,1536]{1,0:T(8,128)(2,1)} %collective-permute-done.8.refs_3_), channel_id=1, source_target_pairs={{0,1},{1,0},{2,3},{3,2},{4,5},{5,4},{6,7},{7,6},{8,9},{9,8},{10,11... | collective-permute-start | bytes 1327112 | tf_op jit(solution)/shard_map/ppermute | solution.py:22
  101.7 24.4 %collective-permute-start.14 = (bf16[128,1536]{1,0:T(8,128)(2,1)S(1)}, bf16[128,1536]{1,0:T(8,128)(2,1)S(1)}, u32[]{:S(2)}, u32[]{:S(2)}) collective-permute-start(bf16[128,1536]{1,0:T(8,128)(2,1)S(1)} %get-tuple-element.118.refs_2_), channel_id=1, source_target_pairs={{0,4},{2,6},{4,0},{6,2},{1,5},{3,7},{5,1},{7,3},{8,12},{10,14},{12... | collective-permute-start | bytes 1179656 | tf_op jit(solution)/shard_map/ppermute | solution.py:27
  104.7 29.3 %collective-permute-start.17 = (bf16[128,1536]{1,0:T(8,128)(2,1)S(1)}, bf16[128,1536]{1,0:T(8,128)(2,1)S(1)}, u32[]{:S(2)}, u32[]{:S(2)}) collective-permute-start(bf16[128,1536]{1,0:T(8,128)(2,1)S(1)} %collective-permute-done.13.refs_2_), channel_id=1, source_target_pairs={{0,1},{1,0},{2,3},{3,2},{4,5},{5,4},{6,7},{7,6},{8,9},{9,8},{10,11... | collective-permute-start | bytes 1179656 | tf_op jit(solution)/shard_map/ppermute | solution.py:22
  105.2 28.8 %collective-permute-start.16 = (bf16[128,1536]{1,0:T(8,128)(2,1)S(1)}, bf16[128,1536]{1,0:T(8,128)(2,1)S(1)}, u32[]{:S(2)}, u32[]{:S(2)}) collective-permute-start(bf16[128,1536]{1,0:T(8,128)(2,1)S(1)} %collective-permute-done.12.refs_0_), channel_id=1, source_target_pairs={{0,1},{1,0},{2,3},{3,2},{4,5},{5,4},{6,7},{7,6},{8,9},{9,8},{10,11... | collective-permute-start | bytes 1179656 | tf_op jit(solution)/shard_map/ppermute | solution.py:22
  156.2 23.5 %collective-permute-start.18 = (bf16[2,144,1536]{2,1,0:T(8,128)(2,1)}, bf16[2,144,1536]{2,1,0:T(8,128)(2,1)S(1)}, u32[]{:S(2)}, u32[]{:S(2)}) collective-permute-start(bf16[2,144,1536]{2,1,0:T(8,128)(2,1)} %get-tuple-element.123), channel_id=1, source_target_pairs={{0,1},{1,0},{2,3},{3,2},{4,5},{5,4},{6,7},{7,6},{8,9},{9,8},{10,11... | collective-permute-start | bytes 2654216 | tf_op jit(solution)/shard_map/ppermute | solution.py:22
  178.0 27.1 %collective-permute-start.19 = (bf16[2,144,1536]{2,1,0:T(8,128)(2,1)}, bf16[2,144,1536]{2,1,0:T(8,128)(2,1)S(1)}, u32[]{:S(2)}, u32[]{:S(2)}) collective-permute-start(bf16[2,144,1536]{2,1,0:T(8,128)(2,1)} %get-tuple-element.133), channel_id=1, source_target_pairs={{0,1},{1,0},{2,3},{3,2},{4,5},{5,4},{6,7},{7,6},{8,9},{9,8},{10,11... | collective-permute-start | bytes 2654216 | tf_op jit(solution)/shard_map/ppermute | solution.py:22
  179.9 25.2 %collective-permute-start.20 = (bf16[144,1536]{1,0:T(8,128)(2,1)S(1)}, bf16[144,1536]{1,0:T(8,128)(2,1)S(1)}, u32[]{:S(2)}, u32[]{:S(2)}) collective-permute-start(bf16[144,1536]{1,0:T(8,128)(2,1)S(1)} %get-tuple-element.124), channel_id=1, source_target_pairs={{0,2},{2,4},{4,6},{6,0},{1,3},{3,5},{5,7},{7,1},{8,10},{10,12},{12... | collective-permute-start | bytes 1327112 | tf_op jit(solution)/shard_map/ppermute | solution.py:32
  183.3 21.8 %collective-permute-start.21 = (bf16[144,1536]{1,0:T(8,128)(2,1)S(1)}, bf16[144,1536]{1,0:T(8,128)(2,1)S(1)}, u32[]{:S(2)}, u32[]{:S(2)}) collective-permute-start(bf16[144,1536]{1,0:T(8,128)(2,1)S(1)} %get-tuple-element.125), channel_id=1, source_target_pairs={{0,6},{2,0},{4,2},{6,4},{1,7},{3,1},{5,3},{7,5},{8,14},{10,8},{12,... | collective-permute-start | bytes 1327112 | tf_op jit(solution)/shard_map/ppermute | solution.py:32
  205.4 195.1 %reduce-scatter.3.cloned.1.call-start = ((), (), s32[]{:S(2)}) async-start(), calls=%async_computation.6 | async-start | bytes 20643840 | tf_op jit(solution)/shard_map/reduce_scatter | solution.py:816
  205.4 33.2 %collective-permute-start.22 = (bf16[4,256,768]{2,1,0:T(8,128)(2,1)}, bf16[4,256,768]{2,1,0:T(8,128)(2,1)}, u32[]{:S(2)}, u32[]{:S(2)}) collective-permute-start(bf16[4,256,768]{2,1,0:T(8,128)(2,1)} %get-tuple-element.144), channel_id=1, source_target_pairs={{0,1},{1,0},{2,3},{3,2},{4,5},{5,4},{6,7},{7,6},{8,9},{9,8},{10,11... | collective-permute-start | bytes 4718600 | tf_op jit(solution)/shard_map/ppermute | solution.py:22
  205.9 36.1 %collective-permute-start.23 = (bf16[144,1536]{1,0:T(8,128)(2,1)S(1)}, bf16[144,1536]{1,0:T(8,128)(2,1)S(1)}, u32[]{:S(2)}, u32[]{:S(2)}) collective-permute-start(bf16[144,1536]{1,0:T(8,128)(2,1)S(1)} %get-tuple-element.143), channel_id=1, source_target_pairs={{0,4},{2,6},{4,0},{6,2},{1,5},{3,7},{5,1},{7,3},{8,12},{10,14},{12... | collective-permute-start | bytes 1327112 | tf_op jit(solution)/shard_map/ppermute | solution.py:32
  242.4 41.8 %all-to-all-start = ((bf16[4,256,768]{2,1,0:T(8,128)(2,1)}), bf16[4,256,768]{2,1,0:T(8,128)(2,1)S(1)}, u32[]{:S(2)}, u32[]{:S(2)}) async-start(bf16[4,256,768]{2,1,0:T(8,128)(2,1)} %add_convert_fusion.1), calls=%async_computation | async-start | bytes 3145728 | tf_op jit(solution)/shard_map/all_to_all | solution.py:53
  284.2 31.0 %all-to-all-start.1 = ((bf16[4,512,256]{2,1,0:T(8,128)(2,1)}), bf16[4,512,256]{2,1,0:T(8,128)(2,1)S(1)}, u32[]{:S(2)}, u32[]{:S(2)}) async-start(bf16[4,512,256]{2,1,0:T(8,128)(2,1)} %get-tuple-element.169), calls=%async_computation.1 | async-start | bytes 2097152 | tf_op jit(solution)/shard_map/all_to_all | solution.py:53
  316.1 61.2 %all-to-all-start.2 = ((bf16[4,2,96,1664]{3,2,1,0:T(8,128)(2,1)}), bf16[4,2,96,1664]{3,2,1,0:T(8,128)(2,1)S(1)}, u32[]{:S(2)}, u32[]{:S(2)}) async-start(bf16[4,2,96,1664]{3,2,1,0:T(8,128)(2,1)} %add_convert_fusion), calls=%async_computation.2 | async-start | bytes 5111808 | tf_op jit(solution)/shard_map/all_to_all | solution.py:53
  325.1 25.6 %collective-permute-start.28 = (bf16[256,1536]{1,0:T(8,128)(2,1)}, bf16[256,1536]{1,0:T(8,128)(2,1)S(1)}, u32[]{:S(2)}, u32[]{:S(2)}) collective-permute-start(bf16[256,1536]{1,0:T(8,128)(2,1)} %get-tuple-element.176), channel_id=1, source_target_pairs={{0,1},{1,0},{2,3},{3,2},{4,5},{5,4},{6,7},{7,6},{8,9},{9,8},{10,11... | collective-permute-start | bytes 2359304 | tf_op jit(solution)/shard_map/ppermute | solution.py:22
  378.8 38.9 %all-to-all-start.3 = ((bf16[8,96,640]{2,1,0:T(8,128)(2,1)}), bf16[8,96,640]{2,1,0:T(8,128)(2,1)S(1)}, u32[]{:S(2)}, u32[]{:S(2)}) async-start(bf16[8,96,640]{2,1,0:T(8,128)(2,1)} %add_convert_fusion.2), calls=%async_computation.3 | async-start | bytes 1966080 | tf_op jit(solution)/shard_map/all_to_all | solution.py:922
  387.0 28.1 %collective-permute-start.30 = (bf16[1,3,384,256]{3,2,1,0:T(8,128)(2,1)}, bf16[1,3,384,256]{3,2,1,0:T(8,128)(2,1)}, u32[]{:S(2)}, u32[]{:S(2)}) collective-permute-start(bf16[1,3,384,256]{3,2,1,0:T(8,128)(2,1)} %fusion.12), channel_id=1, source_target_pairs={{0,16},{8,24},{16,0},{24,8},{1,17},{9,25},{17,1},{25,9},{2,18},{10... | collective-permute-start | bytes 1769480 | tf_op jit(solution)/shard_map/ppermute | solution.py:22
  (58 other events, 700.6 us)
Sparse Core Ops, SparseCore 0:
  205.5 46.0 reduce-scatter.4
  254.4 124.4 reduce-scatter.2
